TPU v7x, 128 devices: a whole 4x4x4 slice. The times are simulated.
128 devices in a mesh: section: 2 (over x_lo), dp: 16 (over y, x_hi, core), tensor: 4 (over z).
Axes of the slice: x: 4 (x_hi: 2, x_lo: 2; x = x_hi * 2 + x_lo), y: 4, z: 4, core: 2. Of those that a mesh axis runs over, the one named last changes fastest.
Arguments:
- inputs: bfloat16 [2, 2048, 1024], P(None, ('dp', 'tensor')), may hold values from -6 to 6
- doc_ids: int32 [2, 2048], P(None, 'dp'), may hold values from -1 to 7, as said below
- cotangent: bfloat16 [2, 2048, 1024], P(None, ('dp', 'tensor')), may hold values from -6 to 6
- w_qkv: bfloat16 [2, 1024, 3, 1024], P('section', None, None, 'tensor'), may hold values from -0.1875 to 0.1875
- b_qv: float32 [2, 2, 1024], P('section', None, 'tensor'), may hold values from -3 to 3
- w_out: bfloat16 [2, 1024, 1024], P('section', 'tensor'), may hold values from -0.75 to 0.75
- b_out: float32 [2, 1024], P('section'), may hold values from -3 to 3
- gain1: float32 [2, 1024], P('section'), may hold values from 0.5 to 1.5
- shift1: float32 [2, 1024], P('section'), may hold values from -1.75 to 1.75
- w_up: bfloat16 [2, 1024, 4096], P('section', None, 'tensor'), may hold values from -0.1875 to 0.1875
- b_up: float32 [2, 4096], P('section', 'tensor'), may hold values from -3 to 3
- w_down: bfloat16 [2, 4096, 1024], P('section', 'tensor'), may hold values from -0.09375 to 0.09375
- b_down: float32 [2, 1024], P('section'), may hold values from -3 to 3
- gain2: float32 [2, 1024], P('section'), may hold values from 0.5 to 1.5
- shift2: float32 [2, 1024], P('section'), may hold values from -1.75 to 1.75
Outputs:
- outputs: bfloat16 [2, 2, 2048, 1024], P('section', None, ('dp', 'tensor'))
- input_grads: float32 [2, 2, 2048, 1024], P('section', None, ('dp', 'tensor'))
- grad_w_qkv: float32 [2, 1024, 3, 1024], P('section', None, None, 'tensor')
- grad_b_qv: float32 [2, 2, 1024], P('section', None, 'tensor')
- grad_w_out: float32 [2, 1024, 1024], P('section', 'tensor')
- grad_b_out: float32 [2, 1024], P('section')
- grad_gain1: float32 [2, 1024], P('section')
- grad_shift1: float32 [2, 1024], P('section')
- grad_w_up: float32 [2, 1024, 4096], P('section', None, 'tensor')
- grad_b_up: float32 [2, 4096], P('section', 'tensor')
- grad_w_down: float32 [2, 4096, 1024], P('section', 'tensor')
- grad_b_down: float32 [2, 1024], P('section')
- grad_gain2: float32 [2, 1024], P('section')
- grad_shift2: float32 [2, 1024], P('section')
Inputs may be any that keep to these rules, and one draw needn't show every extreme that they name: `doc_ids`: within each slot of 128 rows the valid rows come first and their ids rise from 0 in steps of 0 or 1, never above 7; padding rows at the end are -1; at least half of a slot's rows are valid; one slot in every draw is a single sequence of all 128 rows, another holds sequences numbered up to 7, and every slot but the first of these has padding.
All inputs are finite; a program needn't handle non-finite values.
Results may differ from a plain program's by a relative error of at most 0.025.
Values may be sent and summed in bfloat16 or wider, within the bound.
A program may use at most 128 MiB of HBM per device.

v0:
```python
import math

import jax
import jax.numpy as jnp
from jax import lax
from jax.sharding import PartitionSpec as P

HEAD_DIM = 64


def from_behind(x, axis, by):
    count = lax.axis_size(axis)
    pairs = [(i, i + by) for i in range(count) if 0 <= i + by < count]
    return lax.ppermute(x, axis, pairs)


def contract_rows(left, right):
    return lax.dot_general(
        left, right, (((0,), (0,)), ((), ())), preferred_element_type=jnp.float32
    )


def contract_last(left, right):
    return lax.dot_general(
        left, right, (((1,), (1,)), ((), ())), preferred_element_type=jnp.float32
    )


def gelu_slope(upper_pre):
    normal_cdf = 0.5 * (1.0 + lax.erf(upper_pre * (1.0 / math.sqrt(2.0))))
    return normal_cdf + upper_pre * jnp.exp(-0.5 * upper_pre * upper_pre) * (
        1.0 / math.sqrt(2.0 * math.pi)
    )


def normalize(hidden, gain, shift):
    mean_row = jnp.mean(hidden, axis=-1, keepdims=True)
    centred = hidden - mean_row
    inv_std = lax.rsqrt(jnp.mean(centred * centred, axis=-1, keepdims=True) + 1e-05)
    normed = centred * inv_std
    return (normed * gain + shift, normed, inv_std)


def norm_back(grad_out, normed, inv_std, gain):
    scaled = grad_out * gain
    grad_in = inv_std * (
        scaled
        - jnp.mean(scaled, axis=-1, keepdims=True)
        - normed * jnp.mean(scaled * normed, axis=-1, keepdims=True)
    )
    return (grad_in, jnp.sum(grad_out * normed, axis=0), jnp.sum(grad_out, axis=0))


def allowed_mask(slot_docs):
    same_doc = (slot_docs[:, None] == slot_docs[None, :]) & (slot_docs[None, :] >= 0)
    return same_doc | jnp.eye(slot_docs.shape[0], dtype=bool)


def masked_scores(queries, key_heads, allowed):
    raw_scores = jnp.einsum("qhd,khd->hqk", queries, key_heads, preferred_element_type=jnp.float32)
    return jnp.where(allowed[None], raw_scores * HEAD_DIM ** (-0.5), -1e30)


def forward(entry_rows, slot_docs, weights):
    (
        w_joined,
        bias_query,
        bias_value,
        w_attn,
        bias_attn,
        gain_one,
        shift_one,
        w_upper,
        bias_upper,
        w_lower,
        bias_lower,
        gain_two,
        shift_two,
    ) = weights
    local_width = w_attn.shape[0]
    local_heads = local_width // HEAD_DIM
    gathered = lax.all_gather(entry_rows.astype(jnp.bfloat16), "tensor", axis=0, tiled=True)
    slot_rows = gathered.shape[0]
    joined = jnp.dot(gathered, w_joined, preferred_element_type=jnp.float32)
    head_shape = (slot_rows, local_heads, HEAD_DIM)
    queries = (joined[:, :local_width] + bias_query).astype(jnp.bfloat16).reshape(head_shape)
    key_heads = joined[:, local_width : 2 * local_width].astype(jnp.bfloat16).reshape(head_shape)
    values = (joined[:, 2 * local_width :] + bias_value).astype(jnp.bfloat16).reshape(head_shape)
    allowed = allowed_mask(slot_docs)
    scores = masked_scores(queries, key_heads, allowed)
    row_max = jnp.max(scores, axis=-1, keepdims=True)
    exp_scores = jnp.exp(scores - row_max)
    row_total = jnp.sum(exp_scores, axis=-1, keepdims=True)
    attn_probs = (exp_scores / row_total).astype(jnp.bfloat16)
    log_total = row_max + jnp.log(row_total)
    context = jnp.einsum("hqk,khd->qhd", attn_probs, values, preferred_element_type=jnp.float32)
    context = context.reshape(slot_rows, local_width).astype(jnp.bfloat16)
    attn_part = lax.psum_scatter(
        jnp.dot(context, w_attn, preferred_element_type=jnp.float32),
        "tensor",
        scatter_dimension=0,
        tiled=True,
    )
    first_out, normed_one, inv_one = normalize(
        entry_rows + attn_part + bias_attn, gain_one, shift_one
    )
    mid_rows = lax.all_gather(first_out.astype(jnp.bfloat16), "tensor", axis=0, tiled=True)
    upper_pre = jnp.dot(mid_rows, w_upper, preferred_element_type=jnp.float32) + bias_upper
    activation = jax.nn.gelu(upper_pre, approximate=False).astype(jnp.bfloat16)
    mlp_part = lax.psum_scatter(
        jnp.dot(activation, w_lower, preferred_element_type=jnp.float32),
        "tensor",
        scatter_dimension=0,
        tiled=True,
    )
    result, normed_two, inv_two = normalize(first_out + mlp_part + bias_lower, gain_two, shift_two)
    kept_arrays = (
        gathered,
        queries,
        key_heads,
        values,
        log_total,
        context,
        normed_one,
        inv_one,
        mid_rows,
        upper_pre,
        activation,
        normed_two,
        inv_two,
        allowed,
    )
    return (result, kept_arrays)


def mlp_back(grad_out, kept_arrays, weights):
    w_upper, w_lower, gain_two = (weights[7], weights[9], weights[11])
    mid_rows, upper_pre, activation, normed_two, inv_two = kept_arrays[8:13]
    grad_res, grad_gain, grad_shift = norm_back(grad_out, normed_two, inv_two, gain_two)
    grad_bias_lower = jnp.sum(grad_res, axis=0)
    grad_branch = lax.all_gather(grad_res.astype(jnp.bfloat16), "tensor", axis=0, tiled=True)
    grad_w_lower = contract_rows(activation, grad_branch)
    grad_upper = (contract_last(grad_branch, w_lower) * gelu_slope(upper_pre)).astype(jnp.bfloat16)
    grad_bias_upper = jnp.sum(grad_upper.astype(jnp.float32), axis=0)
    grad_w_upper = contract_rows(mid_rows, grad_upper)
    grad_mid = grad_res + lax.psum_scatter(
        contract_last(grad_upper, w_upper).astype(jnp.bfloat16),
        "tensor",
        scatter_dimension=0,
        tiled=True,
    ).astype(jnp.float32)
    return (
        grad_mid,
        (grad_w_upper, grad_bias_upper, grad_w_lower),
        (grad_bias_lower, grad_gain, grad_shift),
    )


def attn_back(grad_mid, kept_arrays, weights):
    w_joined, w_attn, gain_one = (weights[0], weights[3], weights[5])
    gathered, queries, key_heads, values, log_total, context, normed_one, inv_one = kept_arrays[:8]
    allowed = kept_arrays[13]
    slot_rows, local_heads, head_size = queries.shape
    local_width = local_heads * head_size
    grad_res, grad_gain, grad_shift = norm_back(grad_mid, normed_one, inv_one, gain_one)
    grad_bias_attn = jnp.sum(grad_res, axis=0)
    grad_branch = lax.all_gather(grad_res.astype(jnp.bfloat16), "tensor", axis=0, tiled=True)
    grad_w_attn = contract_rows(context, grad_branch)
    grad_context = (
        contract_last(grad_branch, w_attn)
        .astype(jnp.bfloat16)
        .reshape(slot_rows, local_heads, head_size)
    )
    scores = masked_scores(queries, key_heads, allowed)
    soft_probs = jnp.exp(scores - log_total)
    grad_values = jnp.einsum(
        "hqk,qhd->khd",
        soft_probs.astype(jnp.bfloat16),
        grad_context,
        preferred_element_type=jnp.float32,
    )
    grad_probs = jnp.einsum(
        "qhd,khd->hqk", grad_context, values, preferred_element_type=jnp.float32
    )
    grad_scores = soft_probs * (
        grad_probs - jnp.sum(soft_probs * grad_probs, axis=-1, keepdims=True)
    )
    grad_scores = grad_scores.astype(jnp.bfloat16)
    scale_factor = HEAD_DIM ** (-0.5)
    grad_queries = (
        jnp.einsum("hqk,khd->qhd", grad_scores, key_heads, preferred_element_type=jnp.float32)
        * scale_factor
    )
    grad_keys = (
        jnp.einsum("hqk,qhd->khd", grad_scores, queries, preferred_element_type=jnp.float32)
        * scale_factor
    )
    grad_joined = jnp.concatenate(
        [
            grad_queries.reshape(slot_rows, local_width),
            grad_keys.reshape(slot_rows, local_width),
            grad_values.reshape(slot_rows, local_width),
        ],
        axis=1,
    ).astype(jnp.bfloat16)
    joined_wide = grad_joined.astype(jnp.float32)
    grad_bias_qv = jnp.stack(
        [
            jnp.sum(joined_wide[:, :local_width], axis=0),
            jnp.sum(joined_wide[:, 2 * local_width :], axis=0),
        ]
    )
    grad_w_joined = contract_rows(gathered, grad_joined)
    grad_entry = grad_res + lax.psum_scatter(
        contract_last(grad_joined, w_joined).astype(jnp.bfloat16),
        "tensor",
        scatter_dimension=0,
        tiled=True,
    ).astype(jnp.float32)
    return (
        grad_entry,
        (grad_w_joined, grad_bias_qv, grad_w_attn),
        (grad_bias_attn, grad_gain, grad_shift),
    )


def add_all(running, extra):
    if running is None:
        return extra
    return tuple((first_term + second_term for first_term, second_term in zip(running, extra)))


def shards(
    inputs,
    doc_ids,
    cotangent,
    w_qkv,
    b_qv,
    w_out,
    b_out,
    gain1,
    shift1,
    w_up,
    b_up,
    w_down,
    b_down,
    gain2,
    shift2,
):
    batches = inputs.shape[0]
    share_rows = inputs.shape[1]
    model_width = inputs.shape[2]
    weights = (
        w_qkv[0].reshape(model_width, -1),
        b_qv[0, 0],
        b_qv[0, 1],
        w_out[0],
        b_out[0],
        gain1[0],
        shift1[0],
        w_up[0],
        b_up[0],
        w_down[0],
        b_down[0],
        gain2[0],
        shift2[0],
    )
    first_section = lax.axis_index("section") == 0
    blank_rows = jnp.zeros((share_rows, model_width), jnp.float32)
    arrived = blank_rows.astype(jnp.bfloat16)
    results = []
    kept_all = []
    for tick_index in range(batches + 1):
        own_rows = inputs[tick_index].astype(jnp.float32) if tick_index < batches else blank_rows
        entry_rows = jnp.where(first_section, own_rows, arrived.astype(jnp.float32))
        slot_docs = jnp.where(
            first_section, doc_ids[min(tick_index, batches - 1)], doc_ids[max(tick_index - 1, 0)]
        )
        result, kept_arrays = forward(entry_rows, slot_docs, weights)
        sent_rows = result.astype(jnp.bfloat16)
        results.append(sent_rows)
        kept_all.append(kept_arrays)
        if tick_index < batches:
            arrived = from_behind(sent_rows, "section", 1)
    returned = blank_rows.astype(jnp.bfloat16)
    mlp_total = None
    attn_total = None
    small_total = None
    input_list = []
    for back_step in range(batches + 1):
        kept_arrays = kept_all[batches - back_step]
        own_grad = (
            cotangent[batches - 1 - back_step].astype(jnp.float32)
            if back_step < batches
            else blank_rows
        )
        grad_out = jnp.where(first_section, returned.astype(jnp.float32), own_grad)
        grad_mid, mlp_grads, mlp_small = mlp_back(grad_out, kept_arrays, weights)
        mlp_total = add_all(mlp_total, mlp_grads)
        grad_entry, attn_grads, attn_small = attn_back(grad_mid, kept_arrays, weights)
        attn_total = add_all(attn_total, attn_grads)
        small_total = add_all(small_total, mlp_small + attn_small)
        input_list.append(grad_entry)
        if back_step < batches:
            returned = from_behind(grad_entry.astype(jnp.bfloat16), "section", -1)
    summed = (
        lax.psum(mlp_total[0].astype(jnp.bfloat16), "dp").astype(jnp.float32),
        lax.psum(mlp_total[1].astype(jnp.bfloat16), "dp").astype(jnp.float32),
        lax.psum(mlp_total[2].astype(jnp.bfloat16), "dp").astype(jnp.float32),
        lax.psum(attn_total[0].astype(jnp.bfloat16), "dp").astype(jnp.float32),
        lax.psum(attn_total[1].astype(jnp.bfloat16), "dp").astype(jnp.float32),
        lax.psum(attn_total[2].astype(jnp.bfloat16), "dp").astype(jnp.float32),
    )
    mlp_total = summed[:3]
    attn_total = summed[3:]
    small_total = lax.psum(
        (
            small_total[0],
            small_total[1],
            small_total[2],
            small_total[3],
            small_total[4],
            small_total[5],
        ),
        ("dp", "tensor"),
    )
    outputs = jnp.stack(
        [
            jnp.where(first_section, results[index_mb], results[index_mb + 1])
            for index_mb in range(batches)
        ]
    )[None]
    input_grads = jnp.stack(
        [
            jnp.where(
                first_section, input_list[batches - index_mb], input_list[batches - 1 - index_mb]
            )
            for index_mb in range(batches)
        ]
    )[None]
    grad_w_qkv = attn_total[0].reshape(1, model_width, 3, -1)
    return (
        outputs,
        input_grads,
        grad_w_qkv,
        attn_total[1][None],
        attn_total[2][None],
        small_total[3][None],
        small_total[4][None],
        small_total[5][None],
        mlp_total[0][None],
        mlp_total[1][None],
        mlp_total[2][None],
        small_total[0][None],
        small_total[1][None],
        small_total[2][None],
    )


def solution(mesh):
    return jax.shard_map(
        shards,
        mesh=mesh,
        in_specs=(
            P(None, ("dp", "tensor"), None),
            P(None, "dp"),
            P(None, ("dp", "tensor"), None),
            P("section", None, None, "tensor"),
            P("section", None, "tensor"),
            P("section", "tensor", None),
            P("section", None),
            P("section", None),
            P("section", None),
            P("section", None, "tensor"),
            P("section", "tensor"),
            P("section", "tensor", None),
            P("section", None),
            P("section", None),
            P("section", None),
        ),
        out_specs=(
            P("section", None, ("dp", "tensor"), None),
            P("section", None, ("dp", "tensor"), None),
            P("section", None, None, "tensor"),
            P("section", None, "tensor"),
            P("section", "tensor", None),
            P("section", None),
            P("section", None),
            P("section", None),
            P("section", None, "tensor"),
            P("section", "tensor"),
            P("section", "tensor", None),
            P("section", None),
            P("section", None),
            P("section", None),
        ),
        check_vma=False,
    )
```

profile of v0, /device:TPU:1, one launch (start us, length us, event | category | flops | bytes accessed | tf_op | source)
XLA Modules:
  0.0 919.3 jit_solution(16988685143502309106)
XLA Ops:
  11.0 12.3 %all_gather.36 = bf16[128,1024]{1,0:T(8,128)(2,1)S(1)} all-gather(bf16[32,1024]{1,0:T(8,128)(2,1)S(1)} %bitcast_convert_fusion), channel_id=1, replica_groups=mesh['section'=2,'dp'=16,'tensor'=4] {'tensor'}, dimensions={0}, use_global_device_ids=true | all-gather | bytes 327680 | tf_op jit(solution)/shard_map/all_gather | solution.py:82
  23.3 2.7 copy.66
  31.0 23.5 %reduce-scatter.13.cloned.1.call-done = f32[32,1024]{1,0:T(8,128)} async-done(((f32[128,1024]{1,0:T(8,128)}), f32[32,1024]{1,0:T(8,128)}) %reduce-scatter.13.cloned.1.call-update) | async-done | bytes 131088 | tf_op jit(solution)/shard_map/reduce_scatter | solution.py:98
  56.0 9.8 %all_gather.37 = bf16[128,1024]{1,0:T(8,128)(2,1)S(1)} all-gather(bf16[32,1024]{1,0:T(8,128)(2,1)S(1)} %fusion.151), channel_id=1, replica_groups=mesh['section'=2,'dp'=16,'tensor'=4] {'tensor'}, dimensions={0}, use_global_device_ids=true | all-gather | bytes 327680 | tf_op jit(solution)/shard_map/all_gather | solution.py:107
  68.7 2.3 fusion.10
  71.1 23.7 %reduce-scatter.15.cloned.1.call-done = f32[32,1024]{1,0:T(8,128)} async-done(((f32[128,1024]{1,0:T(8,128)}), f32[32,1024]{1,0:T(8,128)}) %reduce-scatter.15.cloned.1.call-update) | async-done | bytes 131088 | tf_op jit(solution)/shard_map/reduce_scatter | solution.py:110
  97.5 3.1 collective-permute-start
  102.7 9.9 %all_gather.38 = bf16[128,1024]{1,0:T(8,128)(2,1)S(1)} all-gather(bf16[32,1024]{1,0:T(8,128)(2,1)S(1)} %fusion.150), channel_id=1, replica_groups=mesh['section'=2,'dp'=16,'tensor'=4] {'tensor'}, dimensions={0}, use_global_device_ids=true | all-gather | bytes 327680 | tf_op jit(solution)/shard_map/all_gather | solution.py:82
  112.5 2.1 fusion.201
  123.7 25.1 %reduce-scatter.17.cloned.1.call-done = f32[32,1024]{1,0:T(8,128)} async-done(((f32[128,1024]{1,0:T(8,128)}), f32[32,1024]{1,0:T(8,128)}) %reduce-scatter.17.cloned.1.call-update) | async-done | bytes 131088 | tf_op jit(solution)/shard_map/reduce_scatter | solution.py:98
  150.7 9.8 %all_gather.39 = bf16[128,1024]{1,0:T(8,128)(2,1)S(1)} all-gather(bf16[32,1024]{1,0:T(8,128)(2,1)S(1)} %fusion.152), channel_id=1, replica_groups=mesh['section'=2,'dp'=16,'tensor'=4] {'tensor'}, dimensions={0}, use_global_device_ids=true | all-gather | bytes 327680 | tf_op jit(solution)/shard_map/all_gather | solution.py:107
  164.0 2.3 fusion.8
  166.3 23.8 %reduce-scatter.19.cloned.1.call-done = f32[32,1024]{1,0:T(8,128)} async-done(((f32[128,1024]{1,0:T(8,128)}), f32[32,1024]{1,0:T(8,128)}) %reduce-scatter.19.cloned.1.call-update) | async-done | bytes 131088 | tf_op jit(solution)/shard_map/reduce_scatter | solution.py:110
  193.0 3.0 collective-permute-start.1
  198.0 9.7 %all_gather.40 = bf16[128,1024]{1,0:T(8,128)(2,1)S(1)} all-gather(bf16[32,1024]{1,0:T(8,128)(2,1)S(1)} %fusion.149), channel_id=1, replica_groups=mesh['section'=2,'dp'=16,'tensor'=4] {'tensor'}, dimensions={0}, use_global_device_ids=true | all-gather | bytes 327680 | tf_op jit(solution)/shard_map/all_gather | solution.py:82
  207.8 2.2 fusion.202
  220.4 25.3 %reduce-scatter.21.cloned.1.call-done = f32[32,1024]{1,0:T(8,128)} async-done(((f32[128,1024]{1,0:T(8,128)}), f32[32,1024]{1,0:T(8,128)}) %reduce-scatter.21.cloned.1.call-update) | async-done | bytes 131088 | tf_op jit(solution)/shard_map/reduce_scatter | solution.py:98
  247.9 9.7 %all_gather.41 = bf16[128,1024]{1,0:T(8,128)(2,1)S(1)} all-gather(bf16[32,1024]{1,0:T(8,128)(2,1)S(1)} %fusion.153), channel_id=1, replica_groups=mesh['section'=2,'dp'=16,'tensor'=4] {'tensor'}, dimensions={0}, use_global_device_ids=true | all-gather | bytes 327680 | tf_op jit(solution)/shard_map/all_gather | solution.py:107
  261.2 2.3 fusion.6
  263.8 23.6 %reduce-scatter.23.cloned.1.call-done = f32[32,1024]{1,0:T(8,128)} async-done(((f32[128,1024]{1,0:T(8,128)}), f32[32,1024]{1,0:T(8,128)}) %reduce-scatter.23.cloned.1.call-update) | async-done | bytes 131088 | tf_op jit(solution)/shard_map/reduce_scatter | solution.py:110
  292.1 9.8 %all_gather.42 = bf16[128,1024]{1,0:T(8,128)(2,1)S(1)} all-gather(bf16[32,1024]{1,0:T(8,128)(2,1)S(1)} %get-tuple-element.68), channel_id=1, replica_groups=mesh['section'=2,'dp'=16,'tensor'=4] {'tensor'}, dimensions={0}, use_global_device_ids=true | all-gather | bytes 327680 | tf_op jit(solution)/shard_map/all_gather | solution.py:141
  302.6 2.5 convert_reduce_fusion.2
  308.8 20.9 %reduce-scatter.25.cloned.1.call-done = bf16[32,1024]{1,0:T(8,128)(2,1)} async-done(((bf16[128,1024]{1,0:T(8,128)(2,1)}), bf16[32,1024]{1,0:T(8,128)(2,1)}) %reduce-scatter.25.cloned.1.call-update) | async-done | bytes 65552 | tf_op jit(solution)/shard_map/reduce_scatter | solution.py:146
  333.8 9.9 %all_gather.43 = bf16[128,1024]{1,0:T(8,128)(2,1)S(1)} all-gather(bf16[32,1024]{1,0:T(8,128)(2,1)S(1)} %convert_element_type.312), channel_id=1, replica_groups=mesh['section'=2,'dp'=16,'tensor'=4] {'tensor'}, dimensions={0}, use_global_device_ids=true | all-gather | bytes 327680 | tf_op jit(solution)/shard_map/all_gather | solution.py:167
  353.3 4.8 fusion.177
  358.1 17.5 %reduce-scatter.27.cloned.1.call-done = bf16[32,1024]{1,0:T(8,128)(2,1)} async-done(((bf16[128,1024]{1,0:T(8,128)(2,1)}), bf16[32,1024]{1,0:T(8,128)(2,1)}) %reduce-scatter.27.cloned.1.call-update) | async-done | bytes 65552 | tf_op jit(solution)/shard_map/reduce_scatter | solution.py:214
  378.0 3.8 fusion.204
  383.3 9.5 %all_gather.44 = bf16[128,1024]{1,0:T(8,128)(2,1)S(1)} all-gather(bf16[32,1024]{1,0:T(8,128)(2,1)S(1)} %get-tuple-element.66), channel_id=1, replica_groups=mesh['section'=2,'dp'=16,'tensor'=4] {'tensor'}, dimensions={0}, use_global_device_ids=true | all-gather | bytes 327680 | tf_op jit(solution)/shard_map/all_gather | solution.py:141
  399.4 4.8 fusion.180
  404.2 17.6 %reduce-scatter.29.cloned.1.call-done = bf16[32,1024]{1,0:T(8,128)(2,1)} async-done(((bf16[128,1024]{1,0:T(8,128)(2,1)}), bf16[32,1024]{1,0:T(8,128)(2,1)}) %reduce-scatter.29.cloned.1.call-update) | async-done | bytes 65552 | tf_op jit(solution)/shard_map/reduce_scatter | solution.py:146
  425.6 9.9 %all_gather.45 = bf16[128,1024]{1,0:T(8,128)(2,1)S(1)} all-gather(bf16[32,1024]{1,0:T(8,128)(2,1)S(1)} %convert_element_type.326), channel_id=1, replica_groups=mesh['section'=2,'dp'=16,'tensor'=4] {'tensor'}, dimensions={0}, use_global_device_ids=true | all-gather | bytes 327680 | tf_op jit(solution)/shard_map/all_gather | solution.py:167
  443.9 3.8 fusion.205
  447.7 2.3 fusion.173
  450.0 16.6 %reduce-scatter.31.cloned.1.call-done = bf16[32,1024]{1,0:T(8,128)(2,1)} async-done(((bf16[128,1024]{1,0:T(8,128)(2,1)}), bf16[32,1024]{1,0:T(8,128)(2,1)}) %reduce-scatter.31.cloned.1.call-update) | async-done | bytes 65552 | tf_op jit(solution)/shard_map/reduce_scatter | solution.py:214
  468.9 2.5 convolution_add_fusion.1
  473.5 10.1 %all_gather.46 = bf16[128,1024]{1,0:T(8,128)(2,1)S(1)} all-gather(bf16[32,1024]{1,0:T(8,128)(2,1)S(1)} %get-tuple-element.64), channel_id=1, replica_groups=mesh['section'=2,'dp'=16,'tensor'=4] {'tensor'}, dimensions={0}, use_global_device_ids=true | all-gather | bytes 327680 | tf_op jit(solution)/shard_map/all_gather | solution.py:141
  486.8 7.1 fusion.25
  495.9 15.2 %reduce-scatter.33.cloned.1.call-done = bf16[32,1024]{1,0:T(8,128)(2,1)} async-done(((bf16[128,1024]{1,0:T(8,128)(2,1)}), bf16[32,1024]{1,0:T(8,128)(2,1)}) %reduce-scatter.33.cloned.1.call-update) | async-done | bytes 65552 | tf_op jit(solution)/shard_map/reduce_scatter | solution.py:146
  514.3 9.9 %all_gather.47 = bf16[128,1024]{1,0:T(8,128)(2,1)S(1)} all-gather(bf16[32,1024]{1,0:T(8,128)(2,1)S(1)} %convert_element_type.338), channel_id=1, replica_groups=mesh['section'=2,'dp'=16,'tensor'=4] {'tensor'}, dimensions={0}, use_global_device_ids=true | all-gather | bytes 327680 | tf_op jit(solution)/shard_map/all_gather | solution.py:167
  529.3 2.2 fusion.171
  531.7 4.6 add_convert_fusion.2
  536.2 2.6 copy.91
  538.8 2.3 fusion.27
  544.5 38.6 %all-reduce.1 = (bf16[1,2,256]{2,1,0:T(2,128)(2,1)S(1)}, bf16[1,1024]{1,0:T(2,128)(2,1)S(1)}) all-reduce(bf16[1,2,256]{2,1,0:T(2,128)(2,1)S(1)} %fusion.166, bf16[1,1024]{1,0:T(2,128)(2,1)S(1)} %broadcast_in_dim.153), channel_id=1, replica_groups=mesh['section'=2,'dp'=16,'tensor'=4] {'dp'}, use_global_device_ids=true, to_apply=%region_52.53 | all-reduce | flops 1536 | bytes 6144 | tf_op jit(solution)/shard_map/psum | solution.py:311
  587.1 314.4 %all-reduce = (f32[1,1024]{1,0:T(1,128)}, f32[1,1024]{1,0:T(1,128)}, f32[1,1024]{1,0:T(1,128)}, f32[1,1024]{1,0:T(1,128)}, f32[1,1024]{1,0:T(1,128)}, /*index=5*/f32[1,1024]{1,0:T(1,128)}) all-reduce(f32[1,1024]{1,0:T(1,128)S(1)} %bitcast.392, ...), channel_id=1, replica_groups=mesh['section'=2,'dp'=16,'tensor'=4] {'dp','tensor'}, use_global_device_ids=true, to_apply=%region_57.58 | all-reduce | flops 6144 | bytes 49152 | tf_op jit(solution)/shard_map/psum | solution.py:316
  903.1 2.2 broadcast_in_dim.147
  907.8 2.5 broadcast_in_dim.152
  910.3 2.5 broadcast_in_dim.156
  (455 shorter events, 126.8 us)
Async XLA Ops:
  7.2 61.5 %copy-start = (bf16[1,1024,1024]{2,1,0:T(8,128)(2,1)S(1)}, bf16[1,1024,1024]{2,1,0:T(8,128)(2,1)}, u32[]{:S(2)}) copy-start(bf16[1,1024,1024]{2,1,0:T(8,128)(2,1)} %param.26) | copy-start | bytes 6291460
  7.2 47.4 %reduce-scatter.13.cloned.1.call-start = ((), (), s32[]{:S(2)}) async-start(), calls=%async_computation.12 | async-start | bytes 655360 | tf_op jit(solution)/shard_map/reduce_scatter | solution.py:98
  10.1 18.0 %copy-start.97 = (f32[1,1,256]{2,1,0:T(1,128)}, f32[1,1,256]{2,1,0:T(1,128)S(1)}, u32[]{:S(2)}) copy-start(f32[1,1,256]{2,1,0:T(1,128)S(1)} %get-tuple-element.94) | copy-start | bytes 3076
  10.1 18.0 %copy-start.99 = (f32[1,1,256]{2,1,0:T(1,128)}, f32[1,1,256]{2,1,0:T(1,128)S(1)}, u32[]{:S(2)}) copy-start(f32[1,1,256]{2,1,0:T(1,128)S(1)} %get-tuple-element.95) | copy-start | bytes 3076
  28.2 26.4 %copy-start.66 = (bf16[2,32,1024]{2,1,0:T(8,128)(2,1)S(1)}, bf16[2,32,1024]{2,1,0:T(8,128)(2,1)}, u32[]{:S(2)}) copy-start(bf16[2,32,1024]{2,1,0:T(8,128)(2,1)} %param.15) | copy-start | bytes 393220
  28.2 26.4 %copy-start.92 = (f32[1,1024]{1,0:T(1,128)S(1)}, f32[1,1024]{1,0:T(1,128)}, u32[]{:S(2)}) copy-start(f32[1,1024]{1,0:T(1,128)} %param.21) | copy-start | bytes 12292
  28.3 27.5 %copy-start.62 = (bf16[128,256]{0,1:T(8,128)(2,1)}, bf16[128,256]{0,1:T(8,128)(2,1)S(1)}, u32[]{:S(2)}) copy-start(bf16[128,256]{0,1:T(8,128)(2,1)S(1)} %copy.68) | copy-start | bytes 196612
  28.3 27.5 %copy-start.61 = (f32[1,1024]{1,0:T(1,128)S(1)}, f32[1,1024]{1,0:T(1,128)}, u32[]{:S(2)}) copy-start(f32[1,1024]{1,0:T(1,128)} %param.22) | copy-start | bytes 12292
  28.4 27.5 %copy-start.88 = (f32[1,1024]{1,0:T(1,128)S(1)}, f32[1,1024]{1,0:T(1,128)}, u32[]{:S(2)}) copy-start(f32[1,1024]{1,0:T(1,128)} %param.23) | copy-start | bytes 12292
  28.5 27.4 %copy-start.63 = (bf16[128,256]{0,1:T(8,128)(2,1)}, bf16[128,256]{0,1:T(8,128)(2,1)S(1)}, u32[]{:S(2)}) copy-start(bf16[128,256]{0,1:T(8,128)(2,1)S(1)} %copy.69) | copy-start | bytes 196612
  28.6 26.0 %copy-start.78 = (bf16[128,256]{0,1:T(8,128)(2,1)}, bf16[128,256]{0,1:T(8,128)(2,1)S(1)}, u32[]{:S(2)}) copy-start(bf16[128,256]{0,1:T(8,128)(2,1)S(1)} %copy.67) | copy-start | bytes 196612
  29.6 26.3 %copy-start.93 = (f32[4,128]{1,0:T(4,128)}, f32[4,128]{1,0:T(4,128)S(1)}, u32[]{:S(2)}) copy-start(f32[4,128]{1,0:T(4,128)S(1)} %get-tuple-element.102) | copy-start | bytes 6148
  29.6 36.2 %copy-start.89 = (f32[1,1024]{1,0:T(1,128)S(1)}, f32[1,1024]{1,0:T(1,128)}, u32[]{:S(2)}) copy-start(f32[1,1024]{1,0:T(1,128)} %param.25) | copy-start | bytes 12292
  29.7 26.2 %copy-start.122 = (f32[4,128]{1,0:T(4,128)}, f32[4,128]{1,0:T(4,128)S(1)}, u32[]{:S(2)}) copy-start(f32[4,128]{1,0:T(4,128)S(1)} %fusion.124) | copy-start | bytes 6148
  29.9 24.7 %copy-start.86 = (bf16[4,64,128]{2,1,0:T(8,128)(2,1)}, bf16[4,64,128]{2,1,0:T(8,128)(2,1)S(1)}, u32[]{:S(2)}) copy-start(bf16[4,64,128]{2,1,0:T(8,128)(2,1)S(1)} %convolution_convert_fusion.11) | copy-start | bytes 196612
  31.0 63.9 %reduce-scatter.15.cloned.1.call-start = ((), (), s32[]{:S(2)}) async-start(), calls=%async_computation.13 | async-start | bytes 655360 | tf_op jit(solution)/shard_map/reduce_scatter | solution.py:110
  68.7 28.0 %copy-start.72 = (f32[1,1024]{1,0:T(1,128)S(1)}, f32[1,1024]{1,0:T(1,128)}, u32[]{:S(2)}) copy-start(f32[1,1024]{1,0:T(1,128)} %param.28) | copy-start | bytes 12292
  71.0 77.8 %reduce-scatter.17.cloned.1.call-start = ((), (), s32[]{:S(2)}) async-start(), calls=%async_computation.14 | async-start | bytes 655360 | tf_op jit(solution)/shard_map/reduce_scatter | solution.py:98
  96.0 95.6 %copy-start.10 = (f32[32,1024]{1,0:T(8,128)}, f32[32,1024]{1,0:T(8,128)S(1)}, u32[]{:S(2)}) copy-start(f32[32,1024]{1,0:T(8,128)S(1)} %get-tuple-element.83) | copy-start | bytes 393220
  97.5 4.5 collective-permute-start
  123.6 66.5 %reduce-scatter.19.cloned.1.call-start = ((), (), s32[]{:S(2)}) async-start(), calls=%async_computation.15 | async-start | bytes 655360 | tf_op jit(solution)/shard_map/reduce_scatter | solution.py:110
  149.9 40.3 %copy-start.12 = (f32[32,1024]{1,0:T(8,128)}, f32[32,1024]{1,0:T(8,128)S(1)}, u32[]{:S(2)}) copy-start(f32[32,1024]{1,0:T(8,128)S(1)} %get-tuple-element.79) | copy-start | bytes 393220
  166.3 79.4 %reduce-scatter.21.cloned.1.call-start = ((), (), s32[]{:S(2)}) async-start(), calls=%async_computation.16 | async-start | bytes 655360 | tf_op jit(solution)/shard_map/reduce_scatter | solution.py:98
  190.1 20.4 %copy-start.98 = (f32[1,1,256]{2,1,0:T(1,128)S(1)}, f32[1,1,256]{2,1,0:T(1,128)}, u32[]{:S(2)}) copy-start(f32[1,1,256]{2,1,0:T(1,128)} %copy-done.97) | copy-start | bytes 3076
  190.1 20.4 %copy-start.100 = (f32[1,1,256]{2,1,0:T(1,128)S(1)}, f32[1,1,256]{2,1,0:T(1,128)}, u32[]{:S(2)}) copy-start(f32[1,1,256]{2,1,0:T(1,128)} %copy-done.99) | copy-start | bytes 3076
  193.0 4.4 collective-permute-start.1
  220.3 67.0 %reduce-scatter.23.cloned.1.call-start = ((), (), s32[]{:S(2)}) async-start(), calls=%async_computation.17 | async-start | bytes 655360 | tf_op jit(solution)/shard_map/reduce_scatter | solution.py:110
  261.2 26.2 %copy-start.90 = (f32[1,1024]{1,0:T(1,128)S(1)}, f32[1,1024]{1,0:T(1,128)}, u32[]{:S(2)}) copy-start(f32[1,1024]{1,0:T(1,128)} %param.27) | copy-start | bytes 12292
  263.5 66.3 %reduce-scatter.25.cloned.1.call-start = ((), (), s32[]{:S(2)}) async-start(), calls=%async_computation.18 | async-start | bytes 327680 | tf_op jit(solution)/shard_map/reduce_scatter | solution.py:146
  307.4 68.3 %reduce-scatter.27.cloned.1.call-start = ((), (), s32[]{:S(2)}) async-start(), calls=%async_computation.19 | async-start | bytes 327680 | tf_op jit(solution)/shard_map/reduce_scatter | solution.py:214
  352.6 69.2 %reduce-scatter.29.cloned.1.call-start = ((), (), s32[]{:S(2)}) async-start(), calls=%async_computation.20 | async-start | bytes 327680 | tf_op jit(solution)/shard_map/reduce_scatter | solution.py:146
  353.3 22.3 %copy-start.34 = (f32[32,1024]{1,0:T(8,128)S(1)}, f32[32,1024]{1,0:T(8,128)}, u32[]{:S(2)}) copy-start(f32[32,1024]{1,0:T(8,128)} %copy-done.33) | copy-start | bytes 393220
  376.6 5.2 collective-permute-start.2
  397.2 69.4 %reduce-scatter.31.cloned.1.call-start = ((), (), s32[]{:S(2)}) async-start(), calls=%async_computation.21 | async-start | bytes 327680 | tf_op jit(solution)/shard_map/reduce_scatter | solution.py:214
  399.4 22.4 %copy-start.13 = (f32[32,1024]{1,0:T(8,128)S(1)}, f32[32,1024]{1,0:T(8,128)}, u32[]{:S(2)}) copy-start(f32[32,1024]{1,0:T(8,128)} %copy-done.12) | copy-start | bytes 393220
  399.4 22.4 %copy-start.39 = (f32[32,1024]{1,0:T(8,128)S(1)}, f32[32,1024]{1,0:T(8,128)}, u32[]{:S(2)}) copy-start(f32[32,1024]{1,0:T(8,128)} %get-tuple-element.67) | copy-start | bytes 393220
  443.8 67.4 %reduce-scatter.33.cloned.1.call-start = ((), (), s32[]{:S(2)}) async-start(), calls=%async_computation.22 | async-start | bytes 327680 | tf_op jit(solution)/shard_map/reduce_scatter | solution.py:146
  450.0 22.6 %copy-start.11 = (f32[32,1024]{1,0:T(8,128)S(1)}, f32[32,1024]{1,0:T(8,128)}, u32[]{:S(2)}) copy-start(f32[32,1024]{1,0:T(8,128)} %copy-done.10) | copy-start | bytes 393220
  450.0 22.6 %copy-start.111 = (f32[32]{0:T(128)S(1)}, f32[32]{0:T(128)}, u32[]{:S(2)}) copy-start(f32[32]{0:T(128)} %copy-done.110) | copy-start | bytes 388
  467.6 5.0 collective-permute-start.3
  486.7 414.8 %reduce-scatter.35.cloned.1.call-start = ((), (), s32[]{:S(2)}) async-start(), calls=%async_computation.23 | async-start | bytes 327680 | tf_op jit(solution)/shard_map/reduce_scatter | solution.py:214
  531.6 371.5 %all-reduce.5.cloned.1.call-start = ((), (), s32[]{:S(2)}) async-start(), calls=%async_computation.24 | async-start | bytes 12582912 | tf_op jit(solution)/shard_map/psum | solution.py:310
  542.1 43.6 %copy-start.102 = (f32[1024]{0:T(1024)S(1)}, f32[1024]{0:T(1024)}, u32[]{:S(2)}) copy-start(f32[1024]{0:T(1024)} %get-tuple-element.24) | copy-start | bytes 12292
  542.1 44.3 %copy-start.101 = (f32[1024]{0:T(1024)S(1)}, f32[1024]{0:T(1024)}, u32[]{:S(2)}) copy-start(f32[1024]{0:T(1024)} %get-tuple-element.60) | copy-start | bytes 12292
  542.1 359.4 %copy-start.35 = (f32[32,1024]{1,0:T(8,128)S(1)}, f32[32,1024]{1,0:T(8,128)}, u32[]{:S(2)}) copy-start(f32[32,1024]{1,0:T(8,128)} %copy-done.33) | copy-start | bytes 393220
  542.1 359.4 %copy-start.37 = (f32[32,1024]{1,0:T(8,128)S(1)}, f32[32,1024]{1,0:T(8,128)}, u32[]{:S(2)}) copy-start(f32[32,1024]{1,0:T(8,128)} %copy-done.36) | copy-start | bytes 393220
  542.1 359.4 %copy-start.82 = (bf16[32,1024]{1,0:T(8,128)(2,1)S(1)}, bf16[32,1024]{1,0:T(8,128)(2,1)}, u32[]{:S(2)}) copy-start(bf16[32,1024]{1,0:T(8,128)(2,1)} %reduce-scatter.27.cloned.1.call-done) | copy-start | bytes 196612
  542.2 359.3 %copy-start.83 = (bf16[32,1024]{1,0:T(8,128)(2,1)S(1)}, bf16[32,1024]{1,0:T(8,128)(2,1)}, u32[]{:S(2)}) copy-start(bf16[32,1024]{1,0:T(8,128)(2,1)} %reduce-scatter.31.cloned.1.call-done) | copy-start | bytes 196612
  (102 other events, 375.3 us)
Sparse Core Ops, SparseCore 0:
  31.1 23.4 reduce-scatter.12
  71.2 23.6 reduce-scatter.14
  123.8 24.9 reduce-scatter.16
  166.4 23.7 reduce-scatter.18
  220.5 25.1 reduce-scatter.20
  263.6 23.6 reduce-scatter.22
  307.5 22.2 reduce-scatter.24
  352.7 22.8 reduce-scatter.26
  397.4 24.4 reduce-scatter.28
  443.9 22.7 reduce-scatter.30
  486.8 24.3 reduce-scatter.32
  531.7 22.7 reduce-scatter.34
  558.4 169.0 all-reduce.4
where the time goes:
time: 931 us; the launch traced here: 919 us
  blocking collectives  473 us (51%)
  waiting for transfers between devices  236 us (25%)
  matrix products  97.3 us (10%)
  other arithmetic  52.9 us (6%)
  local copies, waits for them, and re-layouts  34.8 us (4%)
  between operations  15.5 us (2%)
  starting transfers between devices  9.59 us (1%)
    psum x1, blocking collectives, shards(): lax.psum((small_total[0], small_total[1], small_total[2], small_total[3],...  314 us
    reduce_scatter x3, waiting for transfers between devices, forward(): lax.psum_scatter(jnp.dot(context, w_attn, preferred_element_type=jnp.floa...  74 us
    reduce_scatter x3, waiting for transfers between devices, forward(): lax.psum_scatter(jnp.dot(activation, w_lower, preferred_element_type=jnp....  71.2 us
    reduce_scatter x3, waiting for transfers between devices, mlp_back(): lax.psum_scatter(contract_last(grad_upper, w_upper).astype(jnp.bfloat16),...  53.8 us
    dot_general x12, matrix products, contract_rows(): lax.dot_general(left, right, (((0,), (0,)), ((), ())), preferred_element_...  42.4 us
    psum x1, blocking collectives, shards(): lax.psum(attn_total[1].astype(jnp.bfloat16), 'dp').astype(jnp.float32)  38.6 us
    reduce_scatter x3, waiting for transfers between devices, attn_back(): lax.psum_scatter(contract_last(grad_joined, w_joined).astype(jnp.bfloat16...  34.1 us
    all_gather x3, blocking collectives, forward(): lax.all_gather(entry_rows.astype(jnp.bfloat16), 'tensor', axis=0, tiled=T...  31.9 us
  transfers between devices with their start and end apart: 17, of which 13 were waited for; matrix products, arithmetic and copies ran while one was open for 6% of the time, Pallas kernels for 0%

commit v1 on v0

v1 whole, which is shorter than its diff:
```python
import functools
import math

import jax
import jax.numpy as jnp
from jax import lax
from jax.experimental import pallas as pl
from jax.experimental.pallas import tpu as pltpu
from jax.sharding import PartitionSpec as P

HEAD_DIM = 64
MESH = pl.DeviceIdType.MESH
F32 = jnp.float32
BF16 = jnp.bfloat16
STEP = 256
VMEM_BYTES = 60 * 1024 * 1024


def dot(left, right):
    return lax.dot_general(left, right, (((1,), (0,)), ((), ())), preferred_element_type=F32)


def dot_last(left, right):
    return lax.dot_general(left, right, (((1,), (1,)), ((), ())), preferred_element_type=F32)


def dot_rows(left, right):
    return lax.dot_general(left, right, (((0,), (0,)), ((), ())), preferred_element_type=F32)


def norm(hidden, gain, shift):
    centred = hidden - jnp.mean(hidden, axis=-1, keepdims=True)
    inv_std = lax.rsqrt(jnp.mean(centred * centred, axis=-1, keepdims=True) + 1e-05)
    normed = centred * inv_std
    return normed * gain + shift, normed, inv_std


def norm_back(grad_out, normed, inv_std, gain):
    scaled = grad_out * gain
    return inv_std * (
        scaled
        - jnp.mean(scaled, axis=-1, keepdims=True)
        - normed * jnp.mean(scaled * normed, axis=-1, keepdims=True)
    )


def column_sum(block):
    return jnp.sum(block, axis=0, keepdims=True)


def layer_kernel(
    tensor_size,
    x_ref, doc_ref, cot_ref,
    wqkv_ref, bqv_ref, wout_ref, bout_ref, gain1_ref, shift1_ref,
    wup_ref, bup_ref, wdown_ref, bdown_ref, gain2_ref, shift2_ref,
    out_ref, dx_ref, gqkv_ref, gout_ref, gup_ref, gdown_ref, small_ref,
    gath, rs_send, rs_recv, rs_own,
    qkv, probs, ctx, entry, y1, n1, r1, slope, act, n2, r2, dh2, dh, du, dqkv,
    sent_up, back_in, sent_back, small_acc, small_all,
    ag_ssem, ag_rsem, rs_ssem, rs_rsem, up_ssem, up_rsem, back_ssem, back_rsem,
    small_ssem, small_rsem,
):
    batches, rows, width = x_ref.shape
    slot = rows * tensor_size
    local = wout_ref.shape[0]
    units = wup_ref.shape[1]
    pairs = local // (2 * HEAD_DIM)
    sec = lax.axis_index("section")
    me = lax.axis_index("tensor")
    other = 1 - sec
    scale = HEAD_DIM ** (-0.5)

    barrier = pltpu.get_barrier_semaphore()
    for k in range(1, tensor_size):
        pl.semaphore_signal(
            barrier, inc=1, device_id={"tensor": lax.rem(me + k, tensor_size)}, device_id_type=MESH
        )
    pl.semaphore_signal(barrier, inc=1, device_id={"section": other}, device_id_type=MESH)
    pl.semaphore_wait(barrier, tensor_size)

    def band(index):
        return pl.ds(pl.multiple_of(index * rows, rows), rows)

    mine = band(me)

    def gather_copy(e, m, k):
        return pltpu.make_async_remote_copy(
            src_ref=gath.at[e, m, mine],
            dst_ref=gath.at[e, m, mine],
            send_sem=ag_ssem.at[e, m, k - 1],
            recv_sem=ag_rsem.at[e, m, k - 1],
            device_id={"tensor": lax.rem(me + k, tensor_size)},
            device_id_type=MESH,
        )

    def gather_start(e, m):
        for k in range(1, tensor_size):
            gather_copy(e, m, k).start()

    def gather_wait(e, m):
        for k in range(1, tensor_size):
            source = band(lax.rem(me + tensor_size - k, tensor_size))
            pltpu.make_async_remote_copy(
                src_ref=gath.at[e, m, source],
                dst_ref=gath.at[e, m, source],
                send_sem=ag_ssem.at[e, m, k - 1],
                recv_sem=ag_rsem.at[e, m, k - 1],
                device_id={"tensor": lax.rem(me + k, tensor_size)},
                device_id_type=MESH,
            ).wait_recv()

    def scatter_copy(e, m, k):
        target = lax.rem(me + k, tensor_size)
        return pltpu.make_async_remote_copy(
            src_ref=rs_send.at[e, m, band(target)],
            dst_ref=rs_recv.at[e, m, k - 1],
            send_sem=rs_ssem.at[e, m, k - 1],
            recv_sem=rs_rsem.at[e, m, k - 1],
            device_id={"tensor": target},
            device_id_type=MESH,
        )

    def scatter_start(e, m):
        for k in range(1, tensor_size):
            scatter_copy(e, m, k).start()

    def scatter_wait(e, m):
        total = rs_own[m, mine, :]
        for k in range(1, tensor_size):
            scatter_copy(e, m, k).wait_recv()
        for k in range(1, tensor_size):
            total = total + rs_recv[e, m, k - 1].astype(F32)
        return total

    def put_part(e, m, columns, part):
        rs_own[m, :, columns] = part
        rs_send[e, m, :, columns] = part.astype(BF16)

    def up_copy(m):
        return pltpu.make_async_remote_copy(
            src_ref=sent_up.at[m],
            dst_ref=gath.at[0, m, mine],
            send_sem=up_ssem.at[m],
            recv_sem=up_rsem.at[m],
            device_id={"section": other},
            device_id_type=MESH,
        )

    def back_copy(m):
        return pltpu.make_async_remote_copy(
            src_ref=sent_back.at[m],
            dst_ref=back_in.at[m],
            send_sem=back_ssem.at[m],
            recv_sem=back_rsem.at[m],
            device_id={"section": other},
            device_id_type=MESH,
        )

    def each_batch(body):
        def step(m, carry):
            body(m)
            return carry

        lax.fori_loop(0, batches, step, 0)

    def chunks(total):
        return [pl.ds(c, min(STEP, total - c)) for c in range(0, total, STEP)]

    def head_mask():
        return lax.broadcasted_iota(jnp.int32, (slot, 2 * HEAD_DIM), 1) < HEAD_DIM

    def pick(first, block):
        low_half = head_mask()
        keep = low_half if first else jnp.logical_not(low_half)
        return jnp.where(keep, block, jnp.zeros_like(block))

    small_acc[...] = jnp.zeros_like(small_acc)

    @pl.when(sec == 0)
    def _():
        for m in range(batches):
            gath[0, m, mine, :] = x_ref[m]

    def send_entry(m):
        @pl.when(sec == 1)
        def _():
            up_copy(m).wait_recv()

        gather_start(0, m)

    each_batch(send_entry)

    def attention(m):
        entry[m] = gath[0, m, mine, :].astype(F32)
        gather_wait(0, m)
        for cols in chunks(3 * local):
            part = dot(gath[0, m], wqkv_ref[:, cols])
            if cols.start < local:
                part = part + bqv_ref[0:1, cols]
            elif cols.start >= 2 * local:
                part = part + bqv_ref[1:2, pl.ds(cols.start - 2 * local, cols.size)]
            qkv[m, :, cols] = part.astype(BF16)
        across = jnp.broadcast_to(doc_ref[pl.ds(m, 1), :].astype(F32), (slot, slot))
        down = jnp.transpose(across)
        row_id = lax.broadcasted_iota(jnp.int32, (slot, slot), 0)
        col_id = lax.broadcasted_iota(jnp.int32, (slot, slot), 1)
        allowed = ((across == down) & (across >= 0)) | (row_id == col_id)
        low_half = head_mask()
        for pair in range(pairs):
            at = pair * 2 * HEAD_DIM
            queries = qkv[m, :, pl.ds(at, 2 * HEAD_DIM)]
            key_heads = qkv[m, :, pl.ds(local + at, 2 * HEAD_DIM)]
            values = qkv[m, :, pl.ds(2 * local + at, 2 * HEAD_DIM)]
            halves = []
            for half in range(2):
                raw = dot_last(pick(half == 0, queries), key_heads) * scale
                scores = jnp.where(allowed, raw, -1e30)
                peak = jnp.max(scores, axis=-1, keepdims=True)
                exps = jnp.exp(scores - peak)
                soft = exps / jnp.sum(exps, axis=-1, keepdims=True)
                probs[m, pair * 2 + half] = soft
                halves.append(dot(soft.astype(BF16), values))
            ctx[m, :, pl.ds(at, 2 * HEAD_DIM)] = jnp.where(low_half, halves[0], halves[1]).astype(BF16)
        for cols in chunks(width):
            put_part(0, m, cols, dot(ctx[m], wout_ref[:, cols]))
        scatter_start(0, m)

    each_batch(attention)

    def first_norm(m):
        hidden = entry[m] + scatter_wait(0, m) + bout_ref[...]
        out, normed, inv_std = norm(hidden, gain1_ref[...], shift1_ref[...])
        y1[m], n1[m], r1[m] = out, normed, inv_std
        gath[1, m, mine, :] = out.astype(BF16)
        gather_start(1, m)

    each_batch(first_norm)

    def feed_forward(m):
        gather_wait(1, m)
        for cols in chunks(units):
            pre = dot(gath[1, m], wup_ref[:, cols]) + bup_ref[:, cols]
            cdf = 0.5 * (1.0 + lax.erf(pre * (1.0 / math.sqrt(2.0))))
            slope[m, :, cols] = cdf + pre * jnp.exp(-0.5 * pre * pre) * (
                1.0 / math.sqrt(2.0 * math.pi)
            )
            act[m, :, cols] = (pre * cdf).astype(BF16)
        for cols in chunks(width):
            put_part(1, m, cols, dot(act[m], wdown_ref[:, cols]))
        scatter_start(1, m)

    each_batch(feed_forward)

    def second_norm(m):
        hidden = y1[m] + scatter_wait(1, m) + bdown_ref[...]
        out, normed, inv_std = norm(hidden, gain2_ref[...], shift2_ref[...])
        n2[m], r2[m] = normed, inv_std
        rounded = out.astype(BF16)
        out_ref[m] = rounded

        @pl.when(sec == 0)
        def _():
            sent_up[m] = rounded
            up_copy(m).start()

    each_batch(second_norm)

    def back_entry(m):
        @pl.when(sec == 1)
        def _():
            back_in[m] = cot_ref[m]

        @pl.when(sec == 0)
        def _():
            back_copy(m).wait_recv()

        grad_out = back_in[m].astype(F32)
        grad = norm_back(grad_out, n2[m], r2[m], gain2_ref[...])
        small_acc[0:1, :] += column_sum(grad)
        small_acc[1:2, :] += column_sum(grad_out * n2[m])
        small_acc[2:3, :] += column_sum(grad_out)
        dh2[m] = grad
        gath[2, m, mine, :] = grad.astype(BF16)
        gather_start(2, m)

    each_batch(back_entry)

    def feed_back(m):
        gather_wait(2, m)
        for cols in chunks(units):
            grad = (dot_last(gath[2, m], wdown_ref[cols, :]) * slope[m, :, cols]).astype(BF16)
            du[m, :, cols] = grad
            small_acc[6:7, cols] += column_sum(grad.astype(F32))
        for cols in chunks(width):
            put_part(2, m, cols, dot_last(du[m], wup_ref[cols, :]))
        scatter_start(2, m)

    each_batch(feed_back)

    def weight_grad(left, right, target):
        total = batches * slot
        for rows_at in chunks(left.shape[-1]):
            lhs = left[:, :, rows_at].reshape(total, rows_at.size)
            target[rows_at, :] = dot_rows(lhs, right[...].reshape(total, right.shape[-1])).astype(BF16)

    weight_grad(act, gath.at[2], gdown_ref)
    weight_grad(gath.at[1], du, gup_ref)

    def first_back(m):
        grad_out = dh2[m] + scatter_wait(2, m)
        grad = norm_back(grad_out, n1[m], r1[m], gain1_ref[...])
        small_acc[3:4, :] += column_sum(grad)
        small_acc[4:5, :] += column_sum(grad_out * n1[m])
        small_acc[5:6, :] += column_sum(grad_out)
        dh[m] = grad
        gath[3, m, mine, :] = grad.astype(BF16)
        gather_start(3, m)

    each_batch(first_back)

    def attention_back(m):
        gather_wait(3, m)
        low_half = head_mask()
        for pair in range(pairs):
            at = pair * 2 * HEAD_DIM
            dctx = dot_last(gath[3, m], wout_ref[pl.ds(at, 2 * HEAD_DIM), :]).astype(BF16)
            queries = qkv[m, :, pl.ds(at, 2 * HEAD_DIM)]
            key_heads = qkv[m, :, pl.ds(local + at, 2 * HEAD_DIM)]
            values = qkv[m, :, pl.ds(2 * local + at, 2 * HEAD_DIM)]
            dq, dk, dv = [], [], []
            for half in range(2):
                soft = probs[m, pair * 2 + half]
                dv.append(dot_rows(soft.astype(BF16), dctx))
                dprob = dot_last(pick(half == 0, dctx), values)
                dscore = soft * (dprob - jnp.sum(soft * dprob, axis=-1, keepdims=True))
                dscore = dscore.astype(BF16)
                dq.append(dot(dscore, key_heads) * scale)
                dk.append(dot_rows(dscore, queries) * scale)
            for place, (first, second) in enumerate((dq, dk, dv)):
                cols = pl.ds(place * local + at, 2 * HEAD_DIM)
                grad = jnp.where(low_half, first, second).astype(BF16)
                dqkv[m, :, cols] = grad
                if place != 1:
                    to = at if place == 0 else local + at
                    small_acc[7:8, pl.ds(to, 2 * HEAD_DIM)] += column_sum(grad.astype(F32))
        for cols in chunks(width):
            put_part(3, m, cols, dot_last(dqkv[m], wqkv_ref[cols, :]))
        scatter_start(3, m)

    each_batch(attention_back)

    def small_copy(k, source):
        return pltpu.make_async_remote_copy(
            src_ref=small_all.at[source],
            dst_ref=small_all.at[source],
            send_sem=small_ssem.at[k - 1],
            recv_sem=small_rsem.at[k - 1],
            device_id={"tensor": lax.rem(me + k, tensor_size)},
            device_id_type=MESH,
        )

    small_all[me] = small_acc[...]
    for k in range(1, tensor_size):
        small_copy(k, me).start()

    weight_grad(ctx, gath.at[3], gout_ref)

    def last_back(m):
        grad = dh[m] + scatter_wait(3, m)
        dx_ref[m] = grad

        @pl.when(sec == 1)
        def _():
            sent_back[m] = grad.astype(BF16)
            back_copy(m).start()

    each_batch(last_back)
    weight_grad(gath.at[0], dqkv, gqkv_ref)

    for k in range(1, tensor_size):
        small_copy(k, lax.rem(me + tensor_size - k, tensor_size)).wait_recv()
    total = small_all[0]
    for index in range(1, tensor_size):
        total = total + small_all[index]
    small_row = lax.broadcasted_iota(jnp.int32, total.shape, 0)
    small_ref[...] = jnp.where(small_row < 6, total, small_acc[...])

    for k in range(1, tensor_size):
        small_copy(k, me).wait_send()

    def drain(m):
        for e in range(4):
            for k in range(1, tensor_size):
                gather_copy(e, m, k).wait_send()
                scatter_copy(e, m, k).wait_send()

        @pl.when(sec == 0)
        def _():
            up_copy(m).wait_send()

        @pl.when(sec == 1)
        def _():
            back_copy(m).wait_send()

    each_batch(drain)


def run_layer(x, docs, cot, weights, tensor_size):
    batches, rows, width = x.shape
    slot = rows * tensor_size
    wqkv, bqv, wout, bout, gain1, shift1, wup, bup, wdown, bdown, gain2, shift2 = weights
    local = wout.shape[0]
    units = wup.shape[1]
    heads = local // HEAD_DIM
    vmem = pl.BlockSpec(memory_space=pltpu.VMEM)
    others = tensor_size - 1
    dma = pltpu.SemaphoreType.DMA
    operands = (x, docs, cot) + weights
    small_shape = (8, width)
    shard = (batches, rows, width)
    shapes = (
        jax.ShapeDtypeStruct(shard, BF16),
        jax.ShapeDtypeStruct(shard, F32),
        jax.ShapeDtypeStruct(wqkv.shape, BF16),
        jax.ShapeDtypeStruct(wout.shape, BF16),
        jax.ShapeDtypeStruct(wup.shape, BF16),
        jax.ShapeDtypeStruct(wdown.shape, BF16),
        jax.ShapeDtypeStruct(small_shape, F32),
    )
    scratch = [
        pltpu.VMEM((4, batches, slot, width), BF16),
        pltpu.VMEM((4, batches, slot, width), BF16),
        pltpu.VMEM((4, batches, others, rows, width), BF16),
        pltpu.VMEM((batches, slot, width), F32),
        pltpu.VMEM((batches, slot, 3 * local), BF16),
        pltpu.VMEM((batches, heads, slot, slot), F32),
        pltpu.VMEM((batches, slot, local), BF16),
        pltpu.VMEM(shard, F32),
        pltpu.VMEM(shard, F32),
        pltpu.VMEM(shard, F32),
        pltpu.VMEM((batches, rows, 1), F32),
        pltpu.VMEM((batches, slot, units), F32),
        pltpu.VMEM((batches, slot, units), BF16),
        pltpu.VMEM(shard, F32),
        pltpu.VMEM((batches, rows, 1), F32),
        pltpu.VMEM(shard, F32),
        pltpu.VMEM(shard, F32),
        pltpu.VMEM((batches, slot, units), BF16),
        pltpu.VMEM((batches, slot, 3 * local), BF16),
        pltpu.VMEM(shard, BF16),
        pltpu.VMEM(shard, BF16),
        pltpu.VMEM(shard, BF16),
        pltpu.VMEM(small_shape, F32),
        pltpu.VMEM((tensor_size,) + small_shape, F32),
        dma((4, batches, others)),
        dma((4, batches, others)),
        dma((4, batches, others)),
        dma((4, batches, others)),
        dma((batches,)),
        dma((batches,)),
        dma((batches,)),
        dma((batches,)),
        dma((others,)),
        dma((others,)),
    ]
    return pl.pallas_call(
        functools.partial(layer_kernel, tensor_size),
        out_shape=shapes,
        in_specs=[vmem] * len(operands),
        out_specs=[vmem] * len(shapes),
        scratch_shapes=scratch,
        compiler_params=pltpu.CompilerParams(
            collective_id=0, has_side_effects=True, vmem_limit_bytes=VMEM_BYTES
        ),
        name="layer",
    )(*operands)


AXES = {"core": (1, 2), "x": (2, 2), "y": (4, 4)}
ORDERS = (("core", "x", "y"), ("core", "y", "x"), ("core", "y", "x"), ("core", "x", "y"))


def sum_kernel(count, *refs):
    grads, refs = refs[:count], refs[count:]
    small_in, refs = refs[0], refs[1:]
    outs, refs = refs[:count], refs[count:]
    small_out, refs = refs[0], refs[1:]
    recvs = [refs[c * 3 : c * 3 + 3] for c in range(count)]
    refs = refs[3 * count :]
    sums = [refs[c * 2 : c * 2 + 2] for c in range(count)]
    refs = refs[2 * count :]
    smalls, refs = refs[:3], refs[3:]
    rs_ssem, rs_rsem, ag_ssem, ag_rsem, sm_ssem, sm_rsem = refs
    dp = lax.axis_index("dp")

    def place(axis):
        stride, size = AXES[axis]
        return lax.rem(dp // stride, size)

    def peer(axis, k):
        stride, size = AXES[axis]
        index = lax.rem(place(axis) + k, size)
        return index, {"dp": dp + (index - place(axis)) * stride}

    barrier = pltpu.get_barrier_semaphore()
    greeted = 0
    for axis, (_, size) in AXES.items():
        for k in range(1, size):
            pl.semaphore_signal(barrier, inc=1, device_id=peer(axis, k)[1], device_id_type=MESH)
            greeted += 1
    pl.semaphore_wait(barrier, greeted)

    waits = []

    def small_copy(step, axis, k, source):
        return pltpu.make_async_remote_copy(
            src_ref=smalls[step].at[source],
            dst_ref=smalls[step].at[source],
            send_sem=sm_ssem.at[step, k - 1],
            recv_sem=sm_rsem.at[step, k - 1],
            device_id=peer(axis, k)[1],
            device_id_type=MESH,
        )

    def small_start(step, axis, value):
        smalls[step][place(axis)] = value
        for k in range(1, AXES[axis][1]):
            copy = small_copy(step, axis, k, place(axis))
            copy.start()
            waits.append(copy)

    def small_finish(step, axis):
        size = AXES[axis][1]
        for k in range(1, size):
            small_copy(step, axis, k, lax.rem(place(axis) + size - k, size)).wait_recv()
        total = smalls[step][0]
        for index in range(1, size):
            total = total + smalls[step][index]
        return total

    def rs_copy(c, step, axis, k):
        source = grads[c] if step == 0 else sums[c][step - 1]
        size = AXES[axis][1]
        block = source.shape[0] // size
        index, device = peer(axis, k)
        return pltpu.make_async_remote_copy(
            src_ref=source.at[pl.ds(pl.multiple_of(index * block, block), block)],
            dst_ref=recvs[c][step].at[k - 1],
            send_sem=rs_ssem.at[c, step, k - 1],
            recv_sem=rs_rsem.at[c, step, k - 1],
            device_id=device,
            device_id_type=MESH,
        )

    def rs_start(c, step):
        axis = ORDERS[c][step]
        for k in range(1, AXES[axis][1]):
            copy = rs_copy(c, step, axis, k)
            copy.start()
            waits.append(copy)

    offsets = [[] for _ in range(count)]

    def rs_finish(c, step):
        axis = ORDERS[c][step]
        size = AXES[axis][1]
        source = grads[c] if step == 0 else sums[c][step - 1]
        block = source.shape[0] // size
        for k in range(1, size):
            rs_copy(c, step, axis, k).wait_recv()
        at = pl.multiple_of(place(axis) * block, block)
        total = source[pl.ds(at, block), :].astype(F32)
        for k in range(1, size):
            total = total + recvs[c][step][k - 1].astype(F32)
        base = offsets[c][-1] if step else 0
        offsets[c].append(base + at)
        if step < 2:
            sums[c][step][...] = total.astype(BF16)
        else:
            outs[c][pl.ds(pl.multiple_of(base + at, block), block), :] = total.astype(BF16)

    def block_of(c, step):
        total = outs[c].shape[0]
        for axis in ORDERS[c][: step + 1]:
            total //= AXES[axis][1]
        return total

    def ag_copy(c, step, k, start):
        axis = ORDERS[c][step]
        block = block_of(c, step)
        region = outs[c].at[pl.ds(pl.multiple_of(start, block), block)]
        return pltpu.make_async_remote_copy(
            src_ref=region,
            dst_ref=region,
            send_sem=ag_ssem.at[c, step, k - 1],
            recv_sem=ag_rsem.at[c, step, k - 1],
            device_id=peer(axis, k)[1],
            device_id_type=MESH,
        )

    def ag_start(c, step):
        for k in range(1, AXES[ORDERS[c][step]][1]):
            copy = ag_copy(c, step, k, offsets[c][step])
            copy.start()
            waits.append(copy)

    def ag_finish(c, step):
        axis = ORDERS[c][step]
        size = AXES[axis][1]
        block = block_of(c, step)
        base = offsets[c][step - 1] if step else 0
        for k in range(1, size):
            source = lax.rem(place(axis) + size - k, size)
            ag_copy(c, step, k, base + source * block).wait_recv()

    small_axes = ("core", "y", "x")
    for c in range(count):
        rs_start(c, 0)
    small_start(0, small_axes[0], small_in[...])
    for step in range(3):
        for c in range(count):
            rs_finish(c, step)
            if step < 2:
                rs_start(c, step + 1)
            else:
                ag_start(c, 2)
        total = small_finish(step, small_axes[step])
        if step < 2:
            small_start(step + 1, small_axes[step + 1], total)
        else:
            small_out[...] = total
    for step in (2, 1, 0):
        for c in range(count):
            ag_finish(c, step)
            if step:
                ag_start(c, step - 1)
    for copy in waits:
        copy.wait_send()


def run_sum(grads, small):
    count = len(grads)
    vmem = pl.BlockSpec(memory_space=pltpu.VMEM)
    dma = pltpu.SemaphoreType.DMA
    recvs, sums = [], []
    for grad, order in zip(grads, ORDERS):
        rows = grad.shape[0]
        for step, axis in enumerate(order):
            size = AXES[axis][1]
            rows //= size
            recvs.append(pltpu.VMEM((size - 1, rows, grad.shape[1]), BF16))
            if step < 2:
                sums.append(pltpu.VMEM((rows, grad.shape[1]), BF16))
    smalls = [pltpu.VMEM((AXES[axis][1],) + small.shape, F32) for axis in ("core", "y", "x")]
    shapes = [jax.ShapeDtypeStruct(grad.shape, BF16) for grad in grads]
    shapes.append(jax.ShapeDtypeStruct(small.shape, F32))
    return pl.pallas_call(
        functools.partial(sum_kernel, count),
        out_shape=shapes,
        in_specs=[vmem] * (count + 1),
        out_specs=[vmem] * (count + 1),
        scratch_shapes=recvs + sums + smalls
        + [dma((count, 3, 3)), dma((count, 3, 3)), dma((count, 3, 3)), dma((count, 3, 3))]
        + [dma((3, 3)), dma((3, 3))],
        compiler_params=pltpu.CompilerParams(
            collective_id=1, has_side_effects=True, vmem_limit_bytes=VMEM_BYTES
        ),
        name="sum",
    )(*grads, small)


def shards(
    inputs, doc_ids, cotangent, w_qkv, b_qv, w_out, b_out, gain1, shift1,
    w_up, b_up, w_down, b_down, gain2, shift2,
):
    tensor_size = lax.axis_size("tensor")
    width = inputs.shape[2]
    local = w_out.shape[1]
    weights = (
        w_qkv[0].reshape(width, 3 * local), b_qv[0], w_out[0], b_out, gain1, shift1,
        w_up[0], b_up, w_down[0], b_down, gain2, shift2,
    )
    outputs, input_grads, *grads, small = run_layer(
        inputs, doc_ids, cotangent, weights, tensor_size
    )
    gqkv, gout, gup, gdown, small = run_sum(grads, small)
    return (
        outputs[None],
        input_grads[None],
        gqkv.astype(F32).reshape(1, width, 3, local),
        small[7:8, : 2 * local].reshape(1, 2, local),
        gout.astype(F32)[None],
        small[3:4],
        small[4:5],
        small[5:6],
        gup.astype(F32)[None],
        small[6:7],
        gdown.astype(F32)[None],
        small[0:1],
        small[1:2],
        small[2:3],
    )


def solution(mesh):
    rows = P(None, ("dp", "tensor"), None)
    banked = P("section", None, ("dp", "tensor"), None)
    vector = P("section", None)
    return jax.shard_map(
        shards,
        mesh=mesh,
        in_specs=(
            rows,
            P(None, "dp"),
            rows,
            P("section", None, None, "tensor"),
            P("section", None, "tensor"),
            P("section", "tensor", None),
            vector,
            vector,
            vector,
            P("section", None, "tensor"),
            P("section", "tensor"),
            P("section", "tensor", None),
            vector,
            vector,
            vector,
        ),
        out_specs=(
            banked,
            banked,
            P("section", None, None, "tensor"),
            P("section", None, "tensor"),
            P("section", "tensor", None),
            vector,
            vector,
            vector,
            P("section", None, "tensor"),
            P("section", "tensor"),
            P("section", "tensor", None),
            vector,
            vector,
            vector,
        ),
        check_vma=False,
    )
```

time: 931 us -> 217 us (0.23); the launches traced: 919 us -> 217 us
  blocking collectives: 473 us -> 0 us
  waiting for transfers between devices: 236 us -> 0 us
  Pallas kernels: 0 us -> 197 us
  matrix products: 97.3 us -> 0 us
  other arithmetic: 52.9 us -> 8.79 us
  local copies, waits for them, and re-layouts: 34.8 us -> 9.96 us
  between operations: 15.5 us -> 0.71 us
  starting transfers between devices: 9.59 us -> 0 us
    psum x2 -> x0, blocking collectives: 353 us -> none  [the longest x1 314 us: shards(): lax.psum((small_total[0], small_total[1], small_total[2], small_total[3],...]
    reduce_scatter x12 -> x0, waiting for transfers between devices: 233 us -> none  [the longest x3 74 us: forward(): lax.psum_scatter(jnp.dot(context, w_attn, preferred_element_type=jnp.floa...]
    pallas_call x0 -> x2, Pallas kernels: none -> 197 us  [the longest x1 113 us: run_layer(): pl.pallas_call(functools.partial(layer_kernel, tensor_size), out_shape=sh...]
    all_gather x12 -> x0, blocking collectives: 120 us -> none  [the longest x3 31.9 us: forward(): lax.all_gather(entry_rows.astype(jnp.bfloat16), 'tensor', axis=0, tiled=T...]
    dot_general x54 -> x0, matrix products: 97.3 us -> none  [the longest x12 42.4 us: contract_rows(): lax.dot_general(left, right, (((0,), (0,)), ((), ())), preferred_element_...]
    reduce_sum x28 -> x0, other arithmetic: 21 us -> none  [the longest x6 7.71 us: norm_back(): jnp.sum(grad_out * normed, axis=0)]
    unnamed x267 -> x10, local copies, waits for them, and re-layouts: 18.4 us -> 5.45 us
  transfers between devices with their start and end apart: 17 -> 0, of which waited for: 13 -> 0; matrix products, arithmetic and copies ran while one was open for 6% -> 0% of each run, Pallas kernels for 0% -> 0%
where the time goes in v1:
time: 217 us
  Pallas kernels  197 us (91%)
  local copies, waits for them, and re-layouts  9.96 us (5%)
  other arithmetic  8.79 us (4%)
    pallas_call x1, Pallas kernels, run_layer(): pl.pallas_call(functools.partial(layer_kernel, tensor_size), out_shape=sh...  113 us
    pallas_call x1, Pallas kernels, run_sum(): pl.pallas_call(functools.partial(sum_kernel, count), out_shape=shapes, in...  84.3 us
    broadcast_in_dim x1, other arithmetic, shards(): gdown.astype(F32)[None]  6.67 us
    unnamed x10, local copies, waits for them, and re-layouts  5.45 us

profile of v1, /device:TPU:1, one launch (start us, length us, event | category | flops | bytes accessed | tf_op | source)
XLA Modules:
  0.0 216.7 jit_solution(11025261581680436203)
XLA Ops:
  0.6 1.7 copy.31
  2.4 1.6 copy.32.wqkv_ref
  3.9 113.0 %layer.1 = (bf16[2,32,1024]{2,1,0:T(8,128)(2,1)}, f32[2,32,1024]{2,1,0:T(8,128)}, bf16[1024,768]{1,0:T(8,128)(2,1)}, bf16[256,1024]{1,0:T(8,128)(2,1)}, bf16[102...) custom-call(bf16[2,32,1024]{2,1,0:T(8,128)(2,1)} %x_ref.1, s32[2,128]{1,0:T(2,128)} %doc_ref.1, ...), custom_call_target="tpu_custom_call" | custom-call | tf_op jit(solution)/shard_map/layer/pallas_call | solution.py:466
  117.0 84.3 %sum.1 = (bf16[1024,768]{1,0:T(8,128)(2,1)}, bf16[256,1024]{1,0:T(8,128)(2,1)}, bf16[1024,1024]{1,0:T(8,128)(2,1)}, bf16[1024,1024]{1,0:T(8,128)(2,1)}, f32[8,1024]{1,0:T(8,128)}) custom-call(bf16[1024,768]{1,0:T(8,128)(2,1)} %get-tuple-element.28.refs_0_, bf16[256,1024]{1,0:T(8,128)(2,1)} %get-tuple-element.29.refs_1_, ...), custom_call_target="tpu_custom_call" | custom-call | tf_op jit(solution)/shard_map/sum/pallas_call | solution.py:657
  201.2 0.0 copy-start.2
  201.2 6.7 %bitcast_convert_fusion = (f32[1,1024,1024]{2,1,0:T(8,128)}, f32[1,1024,1024]{2,1,0:T(8,128)}) fusion(bf16[1024,1024]{1,0:T(8,128)(2,1)} %get-tuple-element.37, bf16[1024,1024]{1,0:T(8,128)(2,1)} %get-tuple-element.36), kind=kLoop, calls=%fused_computation | loop fusion | flops 2097152 | bytes 12582912 | tf_op jit(solution)/shard_map/broadcast_in_dim | solution.py:698
  207.9 0.0 copy-done.2
  207.9 0.6 fusion
  208.6 0.6 reshape.39
  209.2 1.7 copy.33
  210.9 0.0 copy-start.1
  210.9 0.0 copy-start
  210.9 2.4 %copy.34 = f32[1,1024,3,256]{3,1,2,0:T(8,128)} copy(f32[1,1024,3,256]{1,3,2,0:T(8,128)S(1)} %bitcast.17) | data formatting | bytes 6291456
  213.2 2.1 bitcast_convert_fusion.2
  215.4 0.0 copy-done.1
  215.4 0.7 copy.37
  216.0 0.0 copy-done
  216.0 0.7 copy.38
  (1 shorter events, 0.0 us)
Async XLA Ops:
  201.2 6.7 %copy-start.2 = (f32[8,1024]{1,0:T(8,128)S(1)}, f32[8,1024]{1,0:T(8,128)}, u32[]{:S(2)}) copy-start(f32[8,1024]{1,0:T(8,128)} %get-tuple-element.34) | copy-start | bytes 98308
  210.9 4.5 %copy-start.1 = (bf16[2,32,1024]{2,1,0:T(8,128)(2,1)S(1)}, bf16[2,32,1024]{2,1,0:T(8,128)(2,1)}, u32[]{:S(2)}) copy-start(bf16[2,32,1024]{2,1,0:T(8,128)(2,1)} %get-tuple-element.26) | copy-start | bytes 393220
  210.9 5.2 %copy-start = (f32[2,32,1024]{2,1,0:T(8,128)S(1)}, f32[2,32,1024]{2,1,0:T(8,128)}, u32[]{:S(2)}) copy-start(f32[2,32,1024]{2,1,0:T(8,128)} %get-tuple-element.27) | copy-start | bytes 786436

commit v2 on v1

--- a/solution.py
+++ b/solution.py
@@ -13,7 +13,36 @@
 F32 = jnp.float32
 BF16 = jnp.bfloat16
 STEP = 256
+SPREAD = ("tensor", "core", "y", "x")
 VMEM_BYTES = 60 * 1024 * 1024
+AXES = {"core": (1, 2), "x": (2, 2), "y": (4, 4)}
+RS_SEM = {"core": 0, "x": 1, "y": 2}
+AG_SEM = {"core": 8, "x": 9, "y": 10}
+X_FIRST = ("core", "x", "y")
+Y_FIRST = ("core", "y", "x")
+
+
+def sum_plan(width, local, units):
+    joined = 3 * width
+    return (
+        ("down", 0, units, width, X_FIRST),
+        ("up", 0, width, units, Y_FIRST),
+        ("out", 0, local, width, Y_FIRST),
+        ("qkv", 0, joined // 2, local, X_FIRST),
+        ("qkv", joined // 2, joined // 2, local, Y_FIRST),
+    )
+
+
+def sum_buffers(rows, columns, order):
+    shapes = []
+    for axis in order:
+        rows //= AXES[axis][1]
+        if axis == "y":
+            shapes.append((8, rows, columns // 2))
+        else:
+            shapes.append((rows, columns))
+        shapes.append((rows, columns))
+    return shapes
 
 
 def dot(left, right):
@@ -48,18 +77,35 @@
     return jnp.sum(block, axis=0, keepdims=True)
 
 
-def layer_kernel(
-    tensor_size,
-    x_ref, doc_ref, cot_ref,
-    wqkv_ref, bqv_ref, wout_ref, bout_ref, gain1_ref, shift1_ref,
-    wup_ref, bup_ref, wdown_ref, bdown_ref, gain2_ref, shift2_ref,
-    out_ref, dx_ref, gqkv_ref, gout_ref, gup_ref, gdown_ref, small_ref,
-    gath, rs_send, rs_recv, rs_own,
-    qkv, probs, ctx, entry, y1, n1, r1, slope, act, n2, r2, dh2, dh, du, dqkv,
-    sent_up, back_in, sent_back, small_acc, small_all,
-    ag_ssem, ag_rsem, rs_ssem, rs_rsem, up_ssem, up_rsem, back_ssem, back_rsem,
-    small_ssem, small_rsem,
-):
+def layer_kernel(tensor_size, plan, *refs):
+    (
+        x_ref, doc_ref, cot_ref,
+        wqkv_hbm, bqv_ref, wout_hbm, bout_ref, gain1_ref, shift1_ref,
+        wup_hbm, bup_ref, wdown_hbm, bdown_ref, gain2_ref, shift2_ref,
+        out_ref, dx_ref, gqkv_ref, gout_ref, gup_ref, gdown_ref, small_ref,
+        wqkv_ref, wout_ref, wup_ref, wdown_ref,
+        gath, rs_send, rs_recv, rs_own,
+        qkv, probs, ctx, entry, y1, n1, r1, slope, act, n2, r2, dh2, dh, du, dqkv,
+        sent_up, back_in, sent_back, small_acc,
+        pqkv, pout, pup, pdown,
+        ag_ssem, ag_rsem, rs_ssem, rs_rsem, up_ssem, up_rsem, back_ssem, back_rsem,
+        sum_ssem, sum_rsem, small_ssem, small_rsem, load_sem,
+        *more,
+    ) = refs
+    spread_refs, sum_refs = more[: len(SPREAD)], more[len(SPREAD) :]
+    grads = {"qkv": pqkv, "out": pout, "up": pup, "down": pdown}
+    totals = {"qkv": gqkv_ref, "out": gout_ref, "up": gup_ref, "down": gdown_ref}
+    loads = [
+        pltpu.make_async_copy(source, target, load_sem.at[index])
+        for index, (source, target) in enumerate(
+            (
+                (wqkv_hbm, wqkv_ref), (wout_hbm, wout_ref),
+                (wup_hbm, wup_ref), (wdown_hbm, wdown_ref),
+            )
+        )
+    ]
+    for load in loads:
+        load.start()
     batches, rows, width = x_ref.shape
     slot = rows * tensor_size
     local = wout_ref.shape[0]
@@ -67,6 +113,7 @@
     pairs = local // (2 * HEAD_DIM)
     sec = lax.axis_index("section")
     me = lax.axis_index("tensor")
+    dp = lax.axis_index("dp")
     other = 1 - sec
     scale = HEAD_DIM ** (-0.5)
 
@@ -76,7 +123,14 @@
             barrier, inc=1, device_id={"tensor": lax.rem(me + k, tensor_size)}, device_id_type=MESH
         )
     pl.semaphore_signal(barrier, inc=1, device_id={"section": other}, device_id_type=MESH)
-    pl.semaphore_wait(barrier, tensor_size)
+    greeted = tensor_size
+    for axis, (stride, size) in AXES.items():
+        for k in range(1, size):
+            index = lax.rem(dp // stride, size)
+            near = dp + (lax.rem(index + k, size) - index) * stride
+            pl.semaphore_signal(barrier, inc=1, device_id={"dp": near}, device_id_type=MESH)
+            greeted += 1
+    pl.semaphore_wait(barrier, greeted)
 
     def band(index):
         return pl.ds(pl.multiple_of(index * rows, rows), rows)
@@ -174,6 +228,218 @@
         keep = low_half if first else jnp.logical_not(low_half)
         return jnp.where(keep, block, jnp.zeros_like(block))
 
+
+    place = {axis: lax.rem(dp // stride, size) for axis, (stride, size) in AXES.items()}
+
+    def dp_peer(axis, k):
+        stride, size = AXES[axis]
+        return {"dp": dp + (lax.rem(place[axis] + k, size) - place[axis]) * stride}
+
+    sends = []
+
+    def send(copy):
+        copy.start()
+        sends.append(copy)
+
+    def sum_events(c):
+        name, first, rows_all, columns, order = plan[c]
+        grad, total = grads[name], totals[name]
+        buffers = sum_refs[6 * c : 6 * c + 6]
+        half = columns // 2
+        low, high = pl.ds(0, half), pl.ds(half, half)
+        sources, starts, blocks = [(grad, first)], [first], [rows_all]
+        for axis in order:
+            blocks.append(blocks[-1] // AXES[axis][1])
+
+        def lines(start, count):
+            return pl.ds(pl.multiple_of(start, count), count)
+
+        def remote(source, target, sem, axis, k):
+            return pltpu.make_async_remote_copy(
+                src_ref=source,
+                dst_ref=target,
+                send_sem=sum_ssem.at[c, sem],
+                recv_sem=sum_rsem.at[c, sem],
+                device_id=dp_peer(axis, k),
+                device_id_type=MESH,
+            )
+
+        def block_at(step, index):
+            ref, base = sources[step]
+            return ref, lines(base + index * blocks[step + 1], blocks[step + 1])
+
+        def add(step, columns_at, parts):
+            ref, at = block_at(step, place[order[step]])
+            value = ref[at, columns_at].astype(F32)
+            for part in parts:
+                value = value + part.astype(F32)
+            return value.astype(BF16)
+
+        def finish(step, pieces):
+            base = starts[step] + place[order[step]] * blocks[step + 1]
+            starts.append(base)
+            for columns_at, value in pieces:
+                if step == 2:
+                    total[lines(base, blocks[3]), columns_at] = value
+                else:
+                    buffers[2 * step + 1][:, columns_at] = value
+            sources.append((buffers[2 * step + 1], 0))
+
+        def pair_scatter(step):
+            axis = order[step]
+            landing = buffers[2 * step]
+
+            def copy():
+                ref, at = block_at(step, 1 - place[axis])
+                return remote(ref.at[at], landing, RS_SEM[axis], axis, 1)
+
+            def begin():
+                send(copy())
+
+            def end():
+                copy().wait_recv()
+                for columns_at in (low, high):
+                    finish_piece = add(step, columns_at, [landing[:, columns_at]])
+                    pieces.append((columns_at, finish_piece))
+                finish(step, pieces)
+
+            pieces = []
+            return [begin, end]
+
+        def ring_scatter(step):
+            landing = buffers[2 * step]
+            here = place["y"]
+
+            def at(k, columns_at):
+                ref, lines_at = block_at(step, lax.rem(here + k, 4))
+                return ref.at[lines_at, columns_at]
+
+            def copy(number):
+                source, k = (
+                    (lambda: at(2, high), 1),
+                    (lambda: at(1, low), 1),
+                    (lambda: at(2, low), 3),
+                    (lambda: at(3, high), 3),
+                    (lambda: landing.at[6], 1),
+                    (lambda: landing.at[7], 3),
+                )[number]
+                return remote(source(), landing.at[number], RS_SEM["y"] + number, "y", k)
+
+            def begin():
+                for number in range(4):
+                    send(copy(number))
+
+            def relay():
+                for number, k, columns_at, out in ((0, 1, high, 4), (2, 3, low, 5)):
+                    copy(number).wait_recv()
+                    value = at(k, columns_at)[...].astype(F32) + landing[number].astype(F32)
+                    landing[out + 2] = value.astype(BF16)
+                    send(copy(out))
+
+            def end():
+                for number in (1, 3, 4, 5):
+                    copy(number).wait_recv()
+                finish(
+                    step,
+                    [
+                        (low, add(step, low, [landing[1], landing[5]])),
+                        (high, add(step, high, [landing[3], landing[4]])),
+                    ],
+                )
+
+            return [begin, relay, end]
+
+        def region(step, index, columns_at=None):
+            at = lines(starts[step] + index * blocks[step + 1], blocks[step + 1])
+            return total.at[at] if columns_at is None else total.at[at, columns_at]
+
+        def pair_gather(step):
+            axis = order[step]
+
+            def copy(index):
+                return remote(region(step, index), region(step, index), AG_SEM[axis], axis, 1)
+
+            return [
+                lambda: send(copy(place[axis])),
+                lambda: copy(1 - place[axis]).wait_recv(),
+            ]
+
+        def ring_gather(step):
+            def copy(number, back):
+                index = lax.rem(place["y"] + 4 - back, 4)
+                columns_at = (None, None, low, high)[number]
+                part = region(step, index, columns_at)
+                return remote(part, part, AG_SEM["y"] + number, "y", (1, 3, 1, 3)[number])
+
+            def begin():
+                send(copy(0, 0))
+                send(copy(1, 0))
+
+            def relay():
+                copy(0, 1).wait_recv()
+                send(copy(2, 1))
+                copy(1, 3).wait_recv()
+                send(copy(3, 3))
+
+            def end():
+                copy(2, 2).wait_recv()
+                copy(3, 2).wait_recv()
+
+            return [begin, relay, end]
+
+        def join(stages):
+            events = [stages[0][0]]
+            for stage, later in zip(stages, stages[1:] + [None]):
+                events.extend(stage[1:-1])
+                if later is None:
+                    events.append(stage[-1])
+                else:
+                    events.append(lambda end=stage[-1], begin=later[0]: (end(), begin()))
+            return events
+
+        scatters = [ring_scatter(i) if a == "y" else pair_scatter(i) for i, a in enumerate(order)]
+        gathers = [ring_gather(i) if a == "y" else pair_gather(i) for i, a in enumerate(order)]
+        return join(scatters + gathers[::-1])
+
+    events = [sum_events(c) for c in range(len(plan))]
+
+    def advance(*which):
+        for c in which:
+            if events[c]:
+                events[c].pop(0)()
+
+    def spread_copy(step, k, source):
+        axis = SPREAD[step]
+        size = tensor_size if axis == "tensor" else AXES[axis][1]
+        at = spread_refs[step].at[source]
+        return pltpu.make_async_remote_copy(
+            src_ref=at,
+            dst_ref=at,
+            send_sem=small_ssem.at[step, k - 1],
+            recv_sem=small_rsem.at[step, k - 1],
+            device_id={"tensor": lax.rem(me + k, size)} if axis == "tensor" else dp_peer(axis, k),
+            device_id_type=MESH,
+        )
+
+    def spread_place(step):
+        axis = SPREAD[step]
+        return (me, tensor_size) if axis == "tensor" else (place[axis], AXES[axis][1])
+
+    def spread_start(step, value):
+        index, size = spread_place(step)
+        spread_refs[step][index] = value
+        for k in range(1, size):
+            send(spread_copy(step, k, index))
+
+    def spread_finish(step):
+        index, size = spread_place(step)
+        for k in range(1, size):
+            spread_copy(step, k, lax.rem(index + size - k, size)).wait_recv()
+        value = spread_refs[step][0]
+        for other_index in range(1, size):
+            value = value + spread_refs[step][other_index]
+        return value
+
     small_acc[...] = jnp.zeros_like(small_acc)
 
     @pl.when(sec == 0)
@@ -181,25 +447,27 @@
         for m in range(batches):
             gath[0, m, mine, :] = x_ref[m]
 
-    def send_entry(m):
+    for m in range(batches):
         @pl.when(sec == 1)
         def _():
             up_copy(m).wait_recv()
 
         gather_start(0, m)
-
-    each_batch(send_entry)
+        if m < batches - 1:
+            for k in range(1, tensor_size):
+                gather_copy(0, m, k).wait_send()
+
+    for load in loads[:2]:
+        load.wait()
 
     def attention(m):
         entry[m] = gath[0, m, mine, :].astype(F32)
         gather_wait(0, m)
-        for cols in chunks(3 * local):
-            part = dot(gath[0, m], wqkv_ref[:, cols])
-            if cols.start < local:
-                part = part + bqv_ref[0:1, cols]
-            elif cols.start >= 2 * local:
-                part = part + bqv_ref[1:2, pl.ds(cols.start - 2 * local, cols.size)]
-            qkv[m, :, cols] = part.astype(BF16)
+        for third in range(3):
+            part = dot(gath[0, m], wqkv_ref[third])
+            if third != 1:
+                part = part + bqv_ref[0, third // 2 : third // 2 + 1, :]
+            qkv[m, :, pl.ds(third * local, local)] = part.astype(BF16)
         across = jnp.broadcast_to(doc_ref[pl.ds(m, 1), :].astype(F32), (slot, slot))
         down = jnp.transpose(across)
         row_id = lax.broadcasted_iota(jnp.int32, (slot, slot), 0)
@@ -236,6 +504,9 @@
 
     each_batch(first_norm)
 
+    for load in loads[2:]:
+        load.wait()
+
     def feed_forward(m):
         gather_wait(1, m)
         for cols in chunks(units):
@@ -297,14 +568,17 @@
 
     each_batch(feed_back)
 
-    def weight_grad(left, right, target):
+    def weight_grad(left, right, target, base=0):
         total = batches * slot
+        rhs = right[...].reshape(total, right.shape[-1])
         for rows_at in chunks(left.shape[-1]):
             lhs = left[:, :, rows_at].reshape(total, rows_at.size)
-            target[rows_at, :] = dot_rows(lhs, right[...].reshape(total, right.shape[-1])).astype(BF16)
-
-    weight_grad(act, gath.at[2], gdown_ref)
-    weight_grad(gath.at[1], du, gup_ref)
+            target[pl.ds(base + rows_at.start, rows_at.size), :] = dot_rows(lhs, rhs).astype(BF16)
+
+    weight_grad(act, gath.at[2], pdown)
+    advance(0)
+    weight_grad(gath.at[1], du, pup)
+    advance(1)
 
     def first_back(m):
         grad_out = dh2[m] + scatter_wait(2, m)
@@ -317,6 +591,8 @@
         gather_start(3, m)
 
     each_batch(first_back)
+
+    advance(0, 1)
 
     def attention_back(m):
         gather_wait(3, m)
@@ -344,26 +620,20 @@
                     to = at if place == 0 else local + at
                     small_acc[7:8, pl.ds(to, 2 * HEAD_DIM)] += column_sum(grad.astype(F32))
         for cols in chunks(width):
-            put_part(3, m, cols, dot_last(dqkv[m], wqkv_ref[cols, :]))
+            part = dot_last(dqkv[m, :, pl.ds(0, local)], wqkv_ref[0, cols, :])
+            for third in range(1, 3):
+                part = part + dot_last(
+                    dqkv[m, :, pl.ds(third * local, local)], wqkv_ref[third, cols, :]
+                )
+            put_part(3, m, cols, part)
         scatter_start(3, m)
 
     each_batch(attention_back)
 
-    def small_copy(k, source):
-        return pltpu.make_async_remote_copy(
-            src_ref=small_all.at[source],
-            dst_ref=small_all.at[source],
-            send_sem=small_ssem.at[k - 1],
-            recv_sem=small_rsem.at[k - 1],
-            device_id={"tensor": lax.rem(me + k, tensor_size)},
-            device_id_type=MESH,
-        )
-
-    small_all[me] = small_acc[...]
-    for k in range(1, tensor_size):
-        small_copy(k, me).start()
-
-    weight_grad(ctx, gath.at[3], gout_ref)
+    spread_start(0, small_acc[...])
+    advance(0, 1)
+    weight_grad(ctx, gath.at[3], pout)
+    advance(2)
 
     def last_back(m):
         grad = dh[m] + scatter_wait(3, m)
@@ -375,24 +645,35 @@
             back_copy(m).start()
 
     each_batch(last_back)
-    weight_grad(gath.at[0], dqkv, gqkv_ref)
-
-    for k in range(1, tensor_size):
-        small_copy(k, lax.rem(me + tensor_size - k, tensor_size)).wait_recv()
-    total = small_all[0]
-    for index in range(1, tensor_size):
-        total = total + small_all[index]
-    small_row = lax.broadcasted_iota(jnp.int32, total.shape, 0)
-    small_ref[...] = jnp.where(small_row < 6, total, small_acc[...])
-
-    for k in range(1, tensor_size):
-        small_copy(k, me).wait_send()
+    for third in range(3):
+        weight_grad(
+            gath.at[0], dqkv.at[:, :, pl.ds(third * local, local)], pqkv, base=third * width
+        )
+    advance(3, 4)
+    advance(0, 1)
+    small_row = lax.broadcasted_iota(jnp.int32, small_acc.shape, 0)
+    spread_start(1, jnp.where(small_row < 6, spread_finish(0), small_acc[...]))
+    small_step = 1
+    while any(events):
+        for c in (2, 3, 4, 0, 1):
+            advance(c)
+        if small_step < len(SPREAD):
+            value = spread_finish(small_step)
+            small_step += 1
+            if small_step < len(SPREAD):
+                spread_start(small_step, value)
+            else:
+                small_ref[...] = value
+
+    for copy in sends:
+        copy.wait_send()
 
     def drain(m):
         for e in range(4):
             for k in range(1, tensor_size):
-                gather_copy(e, m, k).wait_send()
                 scatter_copy(e, m, k).wait_send()
+                if e:
+                    gather_copy(e, m, k).wait_send()
 
         @pl.when(sec == 0)
         def _():
@@ -402,6 +683,8 @@
         def _():
             back_copy(m).wait_send()
 
+    for k in range(1, tensor_size):
+        gather_copy(0, batches - 1, k).wait_send()
     each_batch(drain)
 
 
@@ -421,13 +704,18 @@
     shapes = (
         jax.ShapeDtypeStruct(shard, BF16),
         jax.ShapeDtypeStruct(shard, F32),
-        jax.ShapeDtypeStruct(wqkv.shape, BF16),
+        jax.ShapeDtypeStruct((3 * width, local), BF16),
         jax.ShapeDtypeStruct(wout.shape, BF16),
         jax.ShapeDtypeStruct(wup.shape, BF16),
         jax.ShapeDtypeStruct(wdown.shape, BF16),
         jax.ShapeDtypeStruct(small_shape, F32),
     )
+    plan = sum_plan(width, local, units)
     scratch = [
+        pltpu.VMEM(wqkv.shape, BF16),
+        pltpu.VMEM(wout.shape, BF16),
+        pltpu.VMEM(wup.shape, BF16),
+        pltpu.VMEM(wdown.shape, BF16),
         pltpu.VMEM((4, batches, slot, width), BF16),
         pltpu.VMEM((4, batches, slot, width), BF16),
         pltpu.VMEM((4, batches, others, rows, width), BF16),
@@ -451,7 +739,10 @@
         pltpu.VMEM(shard, BF16),
         pltpu.VMEM(shard, BF16),
         pltpu.VMEM(small_shape, F32),
-        pltpu.VMEM((tensor_size,) + small_shape, F32),
+        pltpu.VMEM((3 * width, local), BF16),
+        pltpu.VMEM(wout.shape, BF16),
+        pltpu.VMEM(wup.shape, BF16),
+        pltpu.VMEM(wdown.shape, BF16),
         dma((4, batches, others)),
         dma((4, batches, others)),
         dma((4, batches, others)),
@@ -460,13 +751,24 @@
         dma((batches,)),
         dma((batches,)),
         dma((batches,)),
-        dma((others,)),
-        dma((others,)),
+        dma((len(plan), 14)),
+        dma((len(plan), 14)),
+        dma((len(SPREAD), 3)),
+        dma((len(SPREAD), 3)),
+        dma((4,)),
     ]
+    for axis in SPREAD:
+        size = tensor_size if axis == "tensor" else AXES[axis][1]
+        scratch.append(pltpu.VMEM((size,) + small_shape, F32))
+    for _, _, rows_all, columns, order in plan:
+        scratch.extend(pltpu.VMEM(shape, BF16) for shape in sum_buffers(rows_all, columns, order))
+    in_specs = [vmem] * len(operands)
+    for index in (3, 5, 9, 11):
+        in_specs[index] = pl.BlockSpec(memory_space=pl.ANY)
     return pl.pallas_call(
-        functools.partial(layer_kernel, tensor_size),
+        functools.partial(layer_kernel, tensor_size, plan),
         out_shape=shapes,
-        in_specs=[vmem] * len(operands),
+        in_specs=in_specs,
         out_specs=[vmem] * len(shapes),
         scratch_shapes=scratch,
         compiler_params=pltpu.CompilerParams(
@@ -474,199 +776,6 @@
         ),
         name="layer",
     )(*operands)
-
-
-AXES = {"core": (1, 2), "x": (2, 2), "y": (4, 4)}
-ORDERS = (("core", "x", "y"), ("core", "y", "x"), ("core", "y", "x"), ("core", "x", "y"))
-
-
-def sum_kernel(count, *refs):
-    grads, refs = refs[:count], refs[count:]
-    small_in, refs = refs[0], refs[1:]
-    outs, refs = refs[:count], refs[count:]
-    small_out, refs = refs[0], refs[1:]
-    recvs = [refs[c * 3 : c * 3 + 3] for c in range(count)]
-    refs = refs[3 * count :]
-    sums = [refs[c * 2 : c * 2 + 2] for c in range(count)]
-    refs = refs[2 * count :]
-    smalls, refs = refs[:3], refs[3:]
-    rs_ssem, rs_rsem, ag_ssem, ag_rsem, sm_ssem, sm_rsem = refs
-    dp = lax.axis_index("dp")
-
-    def place(axis):
-        stride, size = AXES[axis]
-        return lax.rem(dp // stride, size)
-
-    def peer(axis, k):
-        stride, size = AXES[axis]
-        index = lax.rem(place(axis) + k, size)
-        return index, {"dp": dp + (index - place(axis)) * stride}
-
-    barrier = pltpu.get_barrier_semaphore()
-    greeted = 0
-    for axis, (_, size) in AXES.items():
-        for k in range(1, size):
-            pl.semaphore_signal(barrier, inc=1, device_id=peer(axis, k)[1], device_id_type=MESH)
-            greeted += 1
-    pl.semaphore_wait(barrier, greeted)
-
-    waits = []
-
-    def small_copy(step, axis, k, source):
-        return pltpu.make_async_remote_copy(
-            src_ref=smalls[step].at[source],
-            dst_ref=smalls[step].at[source],
-            send_sem=sm_ssem.at[step, k - 1],
-            recv_sem=sm_rsem.at[step, k - 1],
-            device_id=peer(axis, k)[1],
-            device_id_type=MESH,
-        )
-
-    def small_start(step, axis, value):
-        smalls[step][place(axis)] = value
-        for k in range(1, AXES[axis][1]):
-            copy = small_copy(step, axis, k, place(axis))
-            copy.start()
-            waits.append(copy)
-
-    def small_finish(step, axis):
-        size = AXES[axis][1]
-        for k in range(1, size):
-            small_copy(step, axis, k, lax.rem(place(axis) + size - k, size)).wait_recv()
-        total = smalls[step][0]
-        for index in range(1, size):
-            total = total + smalls[step][index]
-        return total
-
-    def rs_copy(c, step, axis, k):
-        source = grads[c] if step == 0 else sums[c][step - 1]
-        size = AXES[axis][1]
-        block = source.shape[0] // size
-        index, device = peer(axis, k)
-        return pltpu.make_async_remote_copy(
-            src_ref=source.at[pl.ds(pl.multiple_of(index * block, block), block)],
-            dst_ref=recvs[c][step].at[k - 1],
-            send_sem=rs_ssem.at[c, step, k - 1],
-            recv_sem=rs_rsem.at[c, step, k - 1],
-            device_id=device,
-            device_id_type=MESH,
-        )
-
-    def rs_start(c, step):
-        axis = ORDERS[c][step]
-        for k in range(1, AXES[axis][1]):
-            copy = rs_copy(c, step, axis, k)
-            copy.start()
-            waits.append(copy)
-
-    offsets = [[] for _ in range(count)]
-
-    def rs_finish(c, step):
-        axis = ORDERS[c][step]
-        size = AXES[axis][1]
-        source = grads[c] if step == 0 else sums[c][step - 1]
-        block = source.shape[0] // size
-        for k in range(1, size):
-            rs_copy(c, step, axis, k).wait_recv()
-        at = pl.multiple_of(place(axis) * block, block)
-        total = source[pl.ds(at, block), :].astype(F32)
-        for k in range(1, size):
-            total = total + recvs[c][step][k - 1].astype(F32)
-        base = offsets[c][-1] if step else 0
-        offsets[c].append(base + at)
-        if step < 2:
-            sums[c][step][...] = total.astype(BF16)
-        else:
-            outs[c][pl.ds(pl.multiple_of(base + at, block), block), :] = total.astype(BF16)
-
-    def block_of(c, step):
-        total = outs[c].shape[0]
-        for axis in ORDERS[c][: step + 1]:
-            total //= AXES[axis][1]
-        return total
-
-    def ag_copy(c, step, k, start):
-        axis = ORDERS[c][step]
-        block = block_of(c, step)
-        region = outs[c].at[pl.ds(pl.multiple_of(start, block), block)]
-        return pltpu.make_async_remote_copy(
-            src_ref=region,
-            dst_ref=region,
-            send_sem=ag_ssem.at[c, step, k - 1],
-            recv_sem=ag_rsem.at[c, step, k - 1],
-            device_id=peer(axis, k)[1],
-            device_id_type=MESH,
-        )
-
-    def ag_start(c, step):
-        for k in range(1, AXES[ORDERS[c][step]][1]):
-            copy = ag_copy(c, step, k, offsets[c][step])
-            copy.start()
-            waits.append(copy)
-
-    def ag_finish(c, step):
-        axis = ORDERS[c][step]
-        size = AXES[axis][1]
-        block = block_of(c, step)
-        base = offsets[c][step - 1] if step else 0
-        for k in range(1, size):
-            source = lax.rem(place(axis) + size - k, size)
-            ag_copy(c, step, k, base + source * block).wait_recv()
-
-    small_axes = ("core", "y", "x")
-    for c in range(count):
-        rs_start(c, 0)
-    small_start(0, small_axes[0], small_in[...])
-    for step in range(3):
-        for c in range(count):
-            rs_finish(c, step)
-            if step < 2:
-                rs_start(c, step + 1)
-            else:
-                ag_start(c, 2)
-        total = small_finish(step, small_axes[step])
-        if step < 2:
-            small_start(step + 1, small_axes[step + 1], total)
-        else:
-            small_out[...] = total
-    for step in (2, 1, 0):
-        for c in range(count):
-            ag_finish(c, step)
-            if step:
-                ag_start(c, step - 1)
-    for copy in waits:
-        copy.wait_send()
-
-
-def run_sum(grads, small):
-    count = len(grads)
-    vmem = pl.BlockSpec(memory_space=pltpu.VMEM)
-    dma = pltpu.SemaphoreType.DMA
-    recvs, sums = [], []
-    for grad, order in zip(grads, ORDERS):
-        rows = grad.shape[0]
-        for step, axis in enumerate(order):
-            size = AXES[axis][1]
-            rows //= size
-            recvs.append(pltpu.VMEM((size - 1, rows, grad.shape[1]), BF16))
-            if step < 2:
-                sums.append(pltpu.VMEM((rows, grad.shape[1]), BF16))
-    smalls = [pltpu.VMEM((AXES[axis][1],) + small.shape, F32) for axis in ("core", "y", "x")]
-    shapes = [jax.ShapeDtypeStruct(grad.shape, BF16) for grad in grads]
-    shapes.append(jax.ShapeDtypeStruct(small.shape, F32))
-    return pl.pallas_call(
-        functools.partial(sum_kernel, count),
-        out_shape=shapes,
-        in_specs=[vmem] * (count + 1),
-        out_specs=[vmem] * (count + 1),
-        scratch_shapes=recvs + sums + smalls
-        + [dma((count, 3, 3)), dma((count, 3, 3)), dma((count, 3, 3)), dma((count, 3, 3))]
-        + [dma((3, 3)), dma((3, 3))],
-        compiler_params=pltpu.CompilerParams(
-            collective_id=1, has_side_effects=True, vmem_limit_bytes=VMEM_BYTES
-        ),
-        name="sum",
-    )(*grads, small)
 
 
 def shards(
@@ -677,17 +786,16 @@
     width = inputs.shape[2]
     local = w_out.shape[1]
     weights = (
-        w_qkv[0].reshape(width, 3 * local), b_qv[0], w_out[0], b_out, gain1, shift1,
+        jnp.transpose(w_qkv[0], (1, 0, 2)), b_qv, w_out[0], b_out, gain1, shift1,
         w_up[0], b_up, w_down[0], b_down, gain2, shift2,
     )
-    outputs, input_grads, *grads, small = run_layer(
+    outputs, input_grads, gqkv, gout, gup, gdown, small = run_layer(
         inputs, doc_ids, cotangent, weights, tensor_size
     )
-    gqkv, gout, gup, gdown, small = run_sum(grads, small)
     return (
         outputs[None],
         input_grads[None],
-        gqkv.astype(F32).reshape(1, width, 3, local),
+        jnp.transpose(gqkv.astype(F32).reshape(3, width, local), (1, 0, 2))[None],
         small[7:8, : 2 * local].reshape(1, 2, local),
         gout.astype(F32)[None],
         small[3:4],

time: 217 us -> 191 us (0.88)
  Pallas kernels: 197 us -> 178 us
  local copies, waits for them, and re-layouts: 9.96 us -> 2.61 us
    pallas_call x2 -> x1, Pallas kernels: 197 us -> 178 us  [run_layer(): pl.pallas_call(functools.partial(layer_kernel, tensor_size, plan), out_sh...]
    unnamed x10 -> x12, local copies, waits for them, and re-layouts: 5.45 us -> 1.38 us
where the time goes in v2:
time: 191 us
  Pallas kernels  178 us (93%)
  other arithmetic  9.8 us (5%)
  local copies, waits for them, and re-layouts  2.61 us (1%)
    pallas_call x1, Pallas kernels, run_layer(): pl.pallas_call(functools.partial(layer_kernel, tensor_size, plan), out_sh...  178 us
    broadcast_in_dim x1, other arithmetic, shards(): gdown.astype(F32)[None]  6.78 us

profile of v2, /device:TPU:1, one launch (start us, length us, event | category | flops | bytes accessed | tf_op | source)
XLA Modules:
  0.0 190.9 jit_solution(11747353659394946407)
XLA Ops:
  0.7 177.8 %layer.1 = (bf16[2,32,1024]{2,1,0:T(8,128)(2,1)}, f32[2,32,1024]{2,1,0:T(8,128)}, bf16[3072,256]{1,0:T(8,128)(2,1)}, bf16[256,1024]{1,0:T(8,128)(2,1)}, bf16[102...) custom-call(bf16[2,32,1024]{2,1,0:T(8,128)(2,1)} %refs_0_.1, s32[2,128]{1,0:T(2,128)} %refs_1_.1, ...), custom_call_target="tpu_custom_call" | custom-call | tf_op jit(solution)/shard_map/layer/pallas_call | solution.py:768
  178.5 0.0 copy-start.4
  178.5 0.0 copy-start
  178.5 6.8 %bitcast_convert_fusion = (f32[1,1024,1024]{2,1,0:T(8,128)}, f32[1,1024,1024]{2,1,0:T(8,128)}) fusion(bf16[1024,1024]{1,0:T(8,128)(2,1)} %get-tuple-element.27, bf16[1024,1024]{1,0:T(8,128)(2,1)} %get-tuple-element.26), kind=kLoop, calls=%fused_computation.1 | loop fusion | flops 2097152 | bytes 12582912 | tf_op jit(solution)/shard_map/broadcast_in_dim | solution.py:806
  185.3 0.0 copy-done.4
  185.3 0.6 fusion
  186.0 0.6 reshape.36
  186.5 0.0 copy-done
  186.6 0.0 copy-start.1
  186.6 0.0 copy-start.3
  186.6 0.0 copy-start.2
  186.6 1.9 %convert_bitcast_fusion = f32[1,1024,3,256]{3,1,2,0:T(8,128)} fusion(bf16[3,1024,256]{2,1,0:T(8,128)(2,1)S(1)} %bitcast.26), kind=kLoop, calls=%fused_computation | loop fusion | flops 786432 | bytes 4718592 | tf_op jit(solution)/shard_map/broadcast_in_dim | solution.py:798
  188.5 0.0 copy-done.1
  188.5 1.1 bitcast_convert_fusion.2
  189.6 0.0 copy-done.3
  189.6 0.7 copy.31
  190.2 0.0 copy-done.2
  190.2 0.7 copy.32
  (1 shorter events, 0.0 us)
Async XLA Ops:
  178.5 6.8 %copy-start.4 = (f32[8,1024]{1,0:T(8,128)S(1)}, f32[8,1024]{1,0:T(8,128)}, u32[]{:S(2)}) copy-start(f32[8,1024]{1,0:T(8,128)} %get-tuple-element.24) | copy-start | bytes 98308
  178.5 8.0 %copy-start = (bf16[3072,256]{1,0:T(8,128)(2,1)S(1)}, bf16[3072,256]{1,0:T(8,128)(2,1)}, u32[]{:S(2)}) copy-start(bf16[3072,256]{1,0:T(8,128)(2,1)} %get-tuple-element.23) | copy-start | bytes 4718596
  186.6 1.9 %copy-start.1 = (bf16[256,1024]{1,0:T(8,128)(2,1)S(1)}, bf16[256,1024]{1,0:T(8,128)(2,1)}, u32[]{:S(2)}) copy-start(bf16[256,1024]{1,0:T(8,128)(2,1)} %get-tuple-element.25) | copy-start | bytes 1572868
  186.6 3.0 %copy-start.3 = (bf16[2,32,1024]{2,1,0:T(8,128)(2,1)S(1)}, bf16[2,32,1024]{2,1,0:T(8,128)(2,1)}, u32[]{:S(2)}) copy-start(bf16[2,32,1024]{2,1,0:T(8,128)(2,1)} %get-tuple-element.21) | copy-start | bytes 393220
  186.6 3.7 %copy-start.2 = (f32[2,32,1024]{2,1,0:T(8,128)S(1)}, f32[2,32,1024]{2,1,0:T(8,128)}, u32[]{:S(2)}) copy-start(f32[2,32,1024]{2,1,0:T(8,128)} %get-tuple-element.22) | copy-start | bytes 786436

commit v3 on v2

--- a/solution.py
+++ b/solution.py
@@ -14,31 +14,39 @@
 BF16 = jnp.bfloat16
 STEP = 256
 SPREAD = ("tensor", "core", "y", "x")
-VMEM_BYTES = 60 * 1024 * 1024
+VMEM_BYTES = 52 * 1024 * 1024
+UNPACK_BYTES = 40 * 1024 * 1024
 AXES = {"core": (1, 2), "x": (2, 2), "y": (4, 4)}
-RS_SEM = {"core": 0, "x": 1, "y": 2}
-AG_SEM = {"core": 8, "x": 9, "y": 10}
-X_FIRST = ("core", "x", "y")
-Y_FIRST = ("core", "y", "x")
+SIZES = {"core": 2, "x": 2, "y": 4, "ring": 4}
+RS_SEM = {"core": 0, "x": 1, "y": 2, "ring": 2}
+AG_SEM = {"core": 8, "x": 9, "y": 10, "ring": 10}
+X_FIRST = ("core", "x", "ring")
+Y_FIRST = ("core", "ring", "x")
+X_FIRST_DIRECT = ("core", "x", "y")
+Y_FIRST_DIRECT = ("core", "y", "x")
 
 
 def sum_plan(width, local, units):
     joined = 3 * width
     return (
-        ("down", 0, units, width, X_FIRST),
-        ("up", 0, width, units, Y_FIRST),
-        ("out", 0, local, width, Y_FIRST),
-        ("qkv", 0, joined // 2, local, X_FIRST),
-        ("qkv", joined // 2, joined // 2, local, Y_FIRST),
+        ("down", 0, units // 2, width, X_FIRST),
+        ("down", units // 2, units // 2, width, Y_FIRST),
+        ("up", 0, width // 2, units, X_FIRST),
+        ("up", width // 2, width // 2, units, Y_FIRST),
+        ("out", 0, local, width, Y_FIRST_DIRECT),
+        ("qkv", 0, joined // 2, local, X_FIRST_DIRECT),
+        ("qkv", joined // 2, joined // 2, local, Y_FIRST_DIRECT),
     )
 
 
 def sum_buffers(rows, columns, order):
     shapes = []
     for axis in order:
-        rows //= AXES[axis][1]
-        if axis == "y":
+        rows //= SIZES[axis]
+        if axis == "ring":
             shapes.append((8, rows, columns // 2))
+        elif axis == "y":
+            shapes.append((3, rows, columns))
         else:
             shapes.append((rows, columns))
         shapes.append((rows, columns))
@@ -210,12 +218,17 @@
             device_id_type=MESH,
         )
 
-    def each_batch(body):
+    def each_batch(body, between=None):
         def step(m, carry):
             body(m)
             return carry
 
-        lax.fori_loop(0, batches, step, 0)
+        if between is None:
+            lax.fori_loop(0, batches, step, 0)
+        else:
+            for m in range(batches):
+                body(m)
+                between(m)
 
     def chunks(total):
         return [pl.ds(c, min(STEP, total - c)) for c in range(0, total, STEP)]
@@ -249,7 +262,7 @@
         low, high = pl.ds(0, half), pl.ds(half, half)
         sources, starts, blocks = [(grad, first)], [first], [rows_all]
         for axis in order:
-            blocks.append(blocks[-1] // AXES[axis][1])
+            blocks.append(blocks[-1] // SIZES[axis])
 
         def lines(start, count):
             return pl.ds(pl.multiple_of(start, count), count)
@@ -264,19 +277,22 @@
                 device_id_type=MESH,
             )
 
+        def spot(step):
+            return place["y" if order[step] == "ring" else order[step]]
+
         def block_at(step, index):
             ref, base = sources[step]
             return ref, lines(base + index * blocks[step + 1], blocks[step + 1])
 
         def add(step, columns_at, parts):
-            ref, at = block_at(step, place[order[step]])
+            ref, at = block_at(step, spot(step))
             value = ref[at, columns_at].astype(F32)
             for part in parts:
                 value = value + part.astype(F32)
             return value.astype(BF16)
 
         def finish(step, pieces):
-            base = starts[step] + place[order[step]] * blocks[step + 1]
+            base = starts[step] + spot(step) * blocks[step + 1]
             starts.append(base)
             for columns_at, value in pieces:
                 if step == 2:
@@ -304,6 +320,28 @@
                 finish(step, pieces)
 
             pieces = []
+            return [begin, end]
+
+        def direct_scatter(step):
+            landing = buffers[2 * step]
+
+            def copy(k):
+                ref, at = block_at(step, lax.rem(place["y"] + k, 4))
+                return remote(ref.at[at], landing.at[k - 1], RS_SEM["y"] + k - 1, "y", k)
+
+            def begin():
+                for k in range(1, 4):
+                    send(copy(k))
+
+            def end():
+                for k in range(1, 4):
+                    copy(k).wait_recv()
+                pieces = []
+                for columns_at in (low, high):
+                    parts = [landing[k, :, columns_at] for k in range(3)]
+                    pieces.append((columns_at, add(step, columns_at, parts)))
+                finish(step, pieces)
+
             return [begin, end]
 
         def ring_scatter(step):
@@ -364,6 +402,21 @@
                 lambda: copy(1 - place[axis]).wait_recv(),
             ]
 
+        def direct_gather(step):
+            def copy(k, back):
+                part = region(step, lax.rem(place["y"] + 4 - back, 4))
+                return remote(part, part, AG_SEM["y"] + k - 1, "y", k)
+
+            def begin():
+                for k in range(1, 4):
+                    send(copy(k, 0))
+
+            def end():
+                for k in range(1, 4):
+                    copy(k, k).wait_recv()
+
+            return [begin, end]
+
         def ring_gather(step):
             def copy(number, back):
                 index = lax.rem(place["y"] + 4 - back, 4)
@@ -397,8 +450,14 @@
                     events.append(lambda end=stage[-1], begin=later[0]: (end(), begin()))
             return events
 
-        scatters = [ring_scatter(i) if a == "y" else pair_scatter(i) for i, a in enumerate(order)]
-        gathers = [ring_gather(i) if a == "y" else pair_gather(i) for i, a in enumerate(order)]
+        forms = {
+            "core": (pair_scatter, pair_gather),
+            "x": (pair_scatter, pair_gather),
+            "y": (direct_scatter, direct_gather),
+            "ring": (ring_scatter, ring_gather),
+        }
+        scatters = [forms[axis][0](step) for step, axis in enumerate(order)]
+        gathers = [forms[axis][1](step) for step, axis in enumerate(order)]
         return join(scatters + gathers[::-1])
 
     events = [sum_events(c) for c in range(len(plan))]
@@ -576,9 +635,9 @@
             target[pl.ds(base + rows_at.start, rows_at.size), :] = dot_rows(lhs, rhs).astype(BF16)
 
     weight_grad(act, gath.at[2], pdown)
-    advance(0)
+    advance(0, 1)
     weight_grad(gath.at[1], du, pup)
-    advance(1)
+    advance(2, 3)
 
     def first_back(m):
         grad_out = dh2[m] + scatter_wait(2, m)
@@ -590,9 +649,7 @@
         gath[3, m, mine, :] = grad.astype(BF16)
         gather_start(3, m)
 
-    each_batch(first_back)
-
-    advance(0, 1)
+    each_batch(first_back, lambda m: advance(0, 1) if m == 0 else advance(2, 3))
 
     def attention_back(m):
         gather_wait(3, m)
@@ -628,12 +685,12 @@
             put_part(3, m, cols, part)
         scatter_start(3, m)
 
-    each_batch(attention_back)
+    each_batch(attention_back, lambda m: advance(1) if m == 0 else None)
 
     spread_start(0, small_acc[...])
+    weight_grad(ctx, gath.at[3], pout)
+    advance(4)
     advance(0, 1)
-    weight_grad(ctx, gath.at[3], pout)
-    advance(2)
 
     def last_back(m):
         grad = dh[m] + scatter_wait(3, m)
@@ -644,19 +701,17 @@
             sent_back[m] = grad.astype(BF16)
             back_copy(m).start()
 
-    each_batch(last_back)
+    each_batch(last_back, lambda m: advance(2, 3, 4) if m == 0 else None)
     for third in range(3):
         weight_grad(
             gath.at[0], dqkv.at[:, :, pl.ds(third * local, local)], pqkv, base=third * width
         )
-    advance(3, 4)
-    advance(0, 1)
+    advance(5, 6)
     small_row = lax.broadcasted_iota(jnp.int32, small_acc.shape, 0)
     spread_start(1, jnp.where(small_row < 6, spread_finish(0), small_acc[...]))
     small_step = 1
     while any(events):
-        for c in (2, 3, 4, 0, 1):
-            advance(c)
+        advance(0, 1, 2, 3, 4, 5, 6)
         if small_step < len(SPREAD):
             value = spread_finish(small_step)
             small_step += 1
@@ -702,13 +757,13 @@
     small_shape = (8, width)
     shard = (batches, rows, width)
     shapes = (
-        jax.ShapeDtypeStruct(shard, BF16),
-        jax.ShapeDtypeStruct(shard, F32),
-        jax.ShapeDtypeStruct((3 * width, local), BF16),
-        jax.ShapeDtypeStruct(wout.shape, BF16),
-        jax.ShapeDtypeStruct(wup.shape, BF16),
-        jax.ShapeDtypeStruct(wdown.shape, BF16),
-        jax.ShapeDtypeStruct(small_shape, F32),
+        pltpu.VMEM(shard, BF16),
+        pltpu.VMEM(shard, F32),
+        pltpu.VMEM((3 * width, local), BF16),
+        pltpu.VMEM(wout.shape, BF16),
+        pltpu.VMEM(wup.shape, BF16),
+        pltpu.VMEM(wdown.shape, BF16),
+        pltpu.VMEM(small_shape, F32),
     )
     plan = sum_plan(width, local, units)
     scratch = [
@@ -778,6 +833,55 @@
     )(*operands)
 
 
+def unpack_kernel(count, *refs):
+    sums, rows_ref, grad_ref, small_ref = refs[:count], *refs[count : count + 3]
+    refs = refs[count + 3 :]
+    targets, rows_out, grad_out, bqv_out, vectors = (
+        refs[:count], refs[count], refs[count + 1], refs[count + 2], refs[count + 3 : count + 10]
+    )
+    wides, sem = refs[count + 10 : count + 10 + count], refs[-1]
+    copies = []
+    for source, target, wide in zip(sums, targets, wides):
+        for at in range(0, source.shape[0], 2 * STEP):
+            rows_at = pl.ds(at, min(2 * STEP, source.shape[0] - at))
+            wide[rows_at, :] = source[rows_at, :].astype(F32)
+            copy = pltpu.make_async_copy(wide.at[rows_at], target.at[rows_at], sem.at[len(copies)])
+            copy.start()
+            copies.append(copy)
+    rows_out[...] = rows_ref[...]
+    grad_out[...] = grad_ref[...]
+    for index, vector in enumerate(vectors):
+        vector[...] = small_ref[index : index + 1, :]
+    half = bqv_out.shape[-1]
+    for index in range(2):
+        bqv_out[0, index : index + 1, :] = small_ref[7:8, pl.ds(index * half, half)]
+    for copy in copies:
+        copy.wait()
+
+
+def unpack(sums, rows, grad, small, local):
+    vmem = pl.BlockSpec(memory_space=pltpu.VMEM)
+    count = len(sums)
+    vector = jax.ShapeDtypeStruct((1, small.shape[1]), F32)
+    wide = [jax.ShapeDtypeStruct(part.shape, F32) for part in sums]
+    shapes = wide + [
+        jax.ShapeDtypeStruct(rows.shape, rows.dtype),
+        jax.ShapeDtypeStruct(grad.shape, grad.dtype),
+        jax.ShapeDtypeStruct((1, 2, local), F32),
+    ] + [vector] * 7
+    pieces = sum(-(-part.shape[0] // (2 * STEP)) for part in sums)
+    return pl.pallas_call(
+        functools.partial(unpack_kernel, count),
+        out_shape=shapes,
+        in_specs=[vmem] * (count + 3),
+        out_specs=[pl.BlockSpec(memory_space=pl.ANY)] * count + [vmem] * 10,
+        scratch_shapes=[pltpu.VMEM(part.shape, F32) for part in sums]
+        + [pltpu.SemaphoreType.DMA((pieces,))],
+        compiler_params=pltpu.CompilerParams(vmem_limit_bytes=UNPACK_BYTES),
+        name="unpack",
+    )(*sums, rows, grad, small)
+
+
 def shards(
     inputs, doc_ids, cotangent, w_qkv, b_qv, w_out, b_out, gain1, shift1,
     w_up, b_up, w_down, b_down, gain2, shift2,
@@ -792,21 +896,25 @@
     outputs, input_grads, gqkv, gout, gup, gdown, small = run_layer(
         inputs, doc_ids, cotangent, weights, tensor_size
     )
+    sums = (gqkv, gout, gup, gdown)
+    gqkv, gout, gup, gdown, outputs, input_grads, gbqv, *vectors = unpack(
+        sums, outputs, input_grads, small, local
+    )
     return (
         outputs[None],
         input_grads[None],
-        jnp.transpose(gqkv.astype(F32).reshape(3, width, local), (1, 0, 2))[None],
-        small[7:8, : 2 * local].reshape(1, 2, local),
-        gout.astype(F32)[None],
-        small[3:4],
-        small[4:5],
-        small[5:6],
-        gup.astype(F32)[None],
-        small[6:7],
-        gdown.astype(F32)[None],
-        small[0:1],
-        small[1:2],
-        small[2:3],
+        jnp.transpose(gqkv.reshape(3, width, local), (1, 0, 2))[None],
+        gbqv,
+        gout[None],
+        vectors[3],
+        vectors[4],
+        vectors[5],
+        gup[None],
+        vectors[6],
+        gdown[None],
+        vectors[0],
+        vectors[1],
+        vectors[2],
     )
 
 

time: 191 us -> 177 us (0.927)
  other arithmetic: 9.8 us -> 0 us
  local copies, waits for them, and re-layouts: 2.61 us -> 0 us
  Pallas kernels: 178 us -> 176 us
    broadcast_in_dim x3 -> x0, other arithmetic: 9.8 us -> none  [the longest x1 6.78 us: shards(): gdown.astype(F32)[None]]
    pallas_call x1, Pallas kernels: 178 us -> 171 us  [run_layer(): pl.pallas_call(functools.partial(layer_kernel, tensor_size, plan), out_sh...]
    pallas_call x0 -> x1, Pallas kernels: none -> 5.5 us  [unpack(): pl.pallas_call(functools.partial(unpack_kernel, count), out_shape=shapes,...]
where the time goes in v3:
time: 177 us
  Pallas kernels  176 us (99%)
    pallas_call x1, Pallas kernels, run_layer(): pl.pallas_call(functools.partial(layer_kernel, tensor_size, plan), out_sh...  171 us
    pallas_call x1, Pallas kernels, unpack(): pl.pallas_call(functools.partial(unpack_kernel, count), out_shape=shapes,...  5.5 us

profile of v3, /device:TPU:1, one launch (start us, length us, event | category | flops | bytes accessed | tf_op | source)
XLA Modules:
  0.0 176.9 jit_solution(5640524650465171215)
XLA Ops:
  0.7 170.7 %layer.1 = (bf16[2,32,1024]{2,1,0:T(8,128)(2,1)S(1)}, f32[2,32,1024]{2,1,0:T(8,128)S(1)}, bf16[3072,256]{1,0:T(8,128)(2,1)S(1)}, bf16[256,1024]{1,0:T(8,128)(2,1...) custom-call(bf16[2,32,1024]{2,1,0:T(8,128)(2,1)} %refs_0_.1, ...), custom_call_target="tpu_custom_call" | custom-call | tf_op jit(solution)/shard_map/layer/pallas_call | solution.py:823
  171.4 5.5 %unpack.1 = (f32[3072,256]{1,0:T(8,128)}, f32[256,1024]{1,0:T(8,128)}, f32[1024,1024]{1,0:T(8,128)}, f32[1024,1024]{1,0:T(8,128)}, bf16[2,32,1024]{2,1,0:T(8,128...) custom-call(bf16[3072,256]{1,0:T(8,128)(2,1)S(1)} %get-tuple-element, ...), custom_call_target="tpu_custom_call" | custom-call | tf_op jit(solution)/shard_map/unpack/pallas_call | solution.py:873

commit v4 on v3

--- a/solution.py
+++ b/solution.py
@@ -16,6 +16,13 @@
 SPREAD = ("tensor", "core", "y", "x")
 VMEM_BYTES = 52 * 1024 * 1024
 UNPACK_BYTES = 40 * 1024 * 1024
+AFTER_FIRST = ((0,), (1, 2))
+AFTER_ATTENTION = ((3,), ())
+AFTER_GRADS = (0, 1, 2)
+AFTER_LAST = ((3, 5, 6), ())
+TAIL = (4, 0, 1, 2, 3, 5, 6, 0, 4, 5, 1, 6, 2, 0, 4, 3, 5, 1, 0, 6, 4, 5, 2, 3, 1, 4, 5, 2, 0, 6, 3, 0, 1, 4, 2, 5, 1, 6, 2, 3, 5, 4, 6, 3, 4, 6)
+TAIL_ONE = (0, 1, 2, 3, 4, 5, 6) * 8
+ROUNDS = 4
 AXES = {"core": (1, 2), "x": (2, 2), "y": (4, 4)}
 SIZES = {"core": 2, "x": 2, "y": 4, "ring": 4}
 RS_SEM = {"core": 0, "x": 1, "y": 2, "ring": 2}
@@ -31,11 +38,11 @@
     return (
         ("down", 0, units // 2, width, X_FIRST),
         ("down", units // 2, units // 2, width, Y_FIRST),
-        ("up", 0, width // 2, units, X_FIRST),
+        ("up", 0, width // 2, units, Y_FIRST),
         ("up", width // 2, width // 2, units, Y_FIRST),
-        ("out", 0, local, width, Y_FIRST_DIRECT),
-        ("qkv", 0, joined // 2, local, X_FIRST_DIRECT),
-        ("qkv", joined // 2, joined // 2, local, Y_FIRST_DIRECT),
+        ("out", 0, local, width, X_FIRST),
+        ("qkv", 0, joined // 2, local, X_FIRST),
+        ("qkv", joined // 2, joined // 2, local, Y_FIRST),
     )
 
 
@@ -91,32 +98,23 @@
         wqkv_hbm, bqv_ref, wout_hbm, bout_ref, gain1_ref, shift1_ref,
         wup_hbm, bup_ref, wdown_hbm, bdown_ref, gain2_ref, shift2_ref,
         out_ref, dx_ref, gqkv_ref, gout_ref, gup_ref, gdown_ref, small_ref,
-        wqkv_ref, wout_ref, wup_ref, wdown_ref,
+        wqkv_ref, wfull, wup_ref, wdown_ref,
         gath, rs_send, rs_recv, rs_own,
         qkv, probs, ctx, entry, y1, n1, r1, slope, act, n2, r2, dh2, dh, du, dqkv,
         sent_up, back_in, sent_back, small_acc,
+        ctx_all, dctx_sent, dctx_all,
         pqkv, pout, pup, pdown,
         ag_ssem, ag_rsem, rs_ssem, rs_rsem, up_ssem, up_rsem, back_ssem, back_rsem,
-        sum_ssem, sum_rsem, small_ssem, small_rsem, load_sem,
+        wide_ssem, wide_rsem, ctx_ssem, ctx_rsem, dctx_ssem, dctx_rsem,
+        sum_ssem, sum_rsem, small_ssem, small_rsem, load_sem, calm_sem,
         *more,
     ) = refs
     spread_refs, sum_refs = more[: len(SPREAD)], more[len(SPREAD) :]
     grads = {"qkv": pqkv, "out": pout, "up": pup, "down": pdown}
     totals = {"qkv": gqkv_ref, "out": gout_ref, "up": gup_ref, "down": gdown_ref}
-    loads = [
-        pltpu.make_async_copy(source, target, load_sem.at[index])
-        for index, (source, target) in enumerate(
-            (
-                (wqkv_hbm, wqkv_ref), (wout_hbm, wout_ref),
-                (wup_hbm, wup_ref), (wdown_hbm, wdown_ref),
-            )
-        )
-    ]
-    for load in loads:
-        load.start()
     batches, rows, width = x_ref.shape
     slot = rows * tensor_size
-    local = wout_ref.shape[0]
+    local = wfull.shape[1]
     units = wup_ref.shape[1]
     pairs = local // (2 * HEAD_DIM)
     sec = lax.axis_index("section")
@@ -124,6 +122,17 @@
     dp = lax.axis_index("dp")
     other = 1 - sec
     scale = HEAD_DIM ** (-0.5)
+    loads = [
+        pltpu.make_async_copy(source, target, load_sem.at[index])
+        for index, (source, target) in enumerate(
+            (
+                (wqkv_hbm, wqkv_ref), (wout_hbm, wfull.at[me]),
+                (wup_hbm, wup_ref), (wdown_hbm, wdown_ref),
+            )
+        )
+    ]
+    for load in loads:
+        load.start()
 
     barrier = pltpu.get_barrier_semaphore()
     for k in range(1, tensor_size):
@@ -194,6 +203,58 @@
             total = total + rs_recv[e, m, k - 1].astype(F32)
         return total
 
+    def share_copy(whole, ssem, rsem, k, source):
+        at = whole.at[source]
+        return pltpu.make_async_remote_copy(
+            src_ref=at,
+            dst_ref=at,
+            send_sem=ssem.at[k - 1],
+            recv_sem=rsem.at[k - 1],
+            device_id={"tensor": lax.rem(me + k, tensor_size)},
+            device_id_type=MESH,
+        )
+
+    def share_start(whole, ssem, rsem):
+        for k in range(1, tensor_size):
+            share_copy(whole, ssem, rsem, k, me).start()
+
+    def share_wait(whole, ssem, rsem):
+        for k in range(1, tensor_size):
+            source = lax.rem(me + tensor_size - k, tensor_size)
+            share_copy(whole, ssem, rsem, k, source).wait_recv()
+
+    def share_drain(whole, ssem, rsem):
+        for k in range(1, tensor_size):
+            share_copy(whole, ssem, rsem, k, me).wait_send()
+
+    wide = (wfull, wide_ssem, wide_rsem)
+
+    def contexts(m):
+        return ctx_all.at[m], ctx_ssem.at[m], ctx_rsem.at[m]
+
+    def dctx_copy(m, k):
+        target = lax.rem(me + k, tensor_size)
+        return pltpu.make_async_remote_copy(
+            src_ref=dctx_sent.at[m, target],
+            dst_ref=dctx_all.at[m, mine],
+            send_sem=dctx_ssem.at[m, k - 1],
+            recv_sem=dctx_rsem.at[m, k - 1],
+            device_id={"tensor": target},
+            device_id_type=MESH,
+        )
+
+    def dctx_wait(m):
+        for k in range(1, tensor_size):
+            source = lax.rem(me + tensor_size - k, tensor_size)
+            pltpu.make_async_remote_copy(
+                src_ref=dctx_sent.at[m, source],
+                dst_ref=dctx_all.at[m, band(source)],
+                send_sem=dctx_ssem.at[m, k - 1],
+                recv_sem=dctx_rsem.at[m, k - 1],
+                device_id={"tensor": source},
+                device_id_type=MESH,
+            ).wait_recv()
+
     def put_part(e, m, columns, part):
         rs_own[m, :, columns] = part
         rs_send[e, m, :, columns] = part.astype(BF16)
@@ -248,21 +309,18 @@
         stride, size = AXES[axis]
         return {"dp": dp + (lax.rem(place[axis] + k, size) - place[axis]) * stride}
 
-    sends = []
-
-    def send(copy):
-        copy.start()
-        sends.append(copy)
-
-    def sum_events(c):
+    def sum_events(c, send):
         name, first, rows_all, columns, order = plan[c]
         grad, total = grads[name], totals[name]
         buffers = sum_refs[6 * c : 6 * c + 6]
         half = columns // 2
         low, high = pl.ds(0, half), pl.ds(half, half)
         sources, starts, blocks = [(grad, first)], [first], [rows_all]
-        for axis in order:
+        for step, axis in enumerate(order):
             blocks.append(blocks[-1] // SIZES[axis])
+            index = place["y" if axis == "ring" else axis]
+            starts.append(starts[-1] + index * blocks[-1])
+            sources.append((buffers[2 * step + 1], 0))
 
         def lines(start, count):
             return pl.ds(pl.multiple_of(start, count), count)
@@ -292,14 +350,11 @@
             return value.astype(BF16)
 
         def finish(step, pieces):
-            base = starts[step] + spot(step) * blocks[step + 1]
-            starts.append(base)
             for columns_at, value in pieces:
                 if step == 2:
-                    total[lines(base, blocks[3]), columns_at] = value
+                    total[lines(starts[3], blocks[3]), columns_at] = value
                 else:
                     buffers[2 * step + 1][:, columns_at] = value
-            sources.append((buffers[2 * step + 1], 0))
 
         def pair_scatter(step):
             axis = order[step]
@@ -310,16 +365,15 @@
                 return remote(ref.at[at], landing, RS_SEM[axis], axis, 1)
 
             def begin():
-                send(copy())
+                send(copy)
 
             def end():
                 copy().wait_recv()
+                pieces = []
                 for columns_at in (low, high):
-                    finish_piece = add(step, columns_at, [landing[:, columns_at]])
-                    pieces.append((columns_at, finish_piece))
+                    pieces.append((columns_at, add(step, columns_at, [landing[:, columns_at]])))
                 finish(step, pieces)
 
-            pieces = []
             return [begin, end]
 
         def direct_scatter(step):
@@ -331,7 +385,7 @@
 
             def begin():
                 for k in range(1, 4):
-                    send(copy(k))
+                    send(functools.partial(copy, k))
 
             def end():
                 for k in range(1, 4):
@@ -365,14 +419,14 @@
 
             def begin():
                 for number in range(4):
-                    send(copy(number))
+                    send(functools.partial(copy, number))
 
             def relay():
                 for number, k, columns_at, out in ((0, 1, high, 4), (2, 3, low, 5)):
                     copy(number).wait_recv()
                     value = at(k, columns_at)[...].astype(F32) + landing[number].astype(F32)
                     landing[out + 2] = value.astype(BF16)
-                    send(copy(out))
+                    send(functools.partial(copy, out))
 
             def end():
                 for number in (1, 3, 4, 5):
@@ -398,7 +452,7 @@
                 return remote(region(step, index), region(step, index), AG_SEM[axis], axis, 1)
 
             return [
-                lambda: send(copy(place[axis])),
+                lambda: send(lambda: copy(place[axis])),
                 lambda: copy(1 - place[axis]).wait_recv(),
             ]
 
@@ -409,7 +463,7 @@
 
             def begin():
                 for k in range(1, 4):
-                    send(copy(k, 0))
+                    send(functools.partial(copy, k, 0))
 
             def end():
                 for k in range(1, 4):
@@ -425,14 +479,14 @@
                 return remote(part, part, AG_SEM["y"] + number, "y", (1, 3, 1, 3)[number])
 
             def begin():
-                send(copy(0, 0))
-                send(copy(1, 0))
+                send(functools.partial(copy, 0, 0))
+                send(functools.partial(copy, 1, 0))
 
             def relay():
                 copy(0, 1).wait_recv()
-                send(copy(2, 1))
+                send(functools.partial(copy, 2, 1))
                 copy(1, 3).wait_recv()
-                send(copy(3, 3))
+                send(functools.partial(copy, 3, 3))
 
             def end():
                 copy(2, 2).wait_recv()
@@ -460,12 +514,21 @@
         gathers = [forms[axis][1](step) for step, axis in enumerate(order)]
         return join(scatters + gathers[::-1])
 
-    events = [sum_events(c) for c in range(len(plan))]
-
-    def advance(*which):
-        for c in which:
-            if events[c]:
-                events[c].pop(0)()
+    sends, events = ([], []), ([], [])
+    for section in range(2):
+
+        def send(make, section=section):
+            make().start()
+            sends[section].append(make)
+
+        events[section].extend(sum_events(c, send) for c in range(len(plan)))
+
+    def advance(section, *which):
+        @pl.when(sec == section)
+        def _():
+            for c in which:
+                if events[section][c]:
+                    events[section][c].pop(0)()
 
     def spread_copy(step, k, source):
         axis = SPREAD[step]
@@ -488,7 +551,7 @@
         index, size = spread_place(step)
         spread_refs[step][index] = value
         for k in range(1, size):
-            send(spread_copy(step, k, index))
+            spread_copy(step, k, index).start()
 
     def spread_finish(step):
         index, size = spread_place(step)
@@ -506,6 +569,12 @@
         for m in range(batches):
             gath[0, m, mine, :] = x_ref[m]
 
+    loads[1].wait()
+
+    @pl.when(sec == 1)
+    def _():
+        share_start(*wide)
+
     for m in range(batches):
         @pl.when(sec == 1)
         def _():
@@ -516,8 +585,12 @@
             for k in range(1, tensor_size):
                 gather_copy(0, m, k).wait_send()
 
-    for load in loads[:2]:
-        load.wait()
+    loads[0].wait()
+
+    @pl.when(sec == 1)
+    def _():
+        share_wait(*wide)
+
 
     def attention(m):
         entry[m] = gath[0, m, mine, :].astype(F32)
@@ -548,26 +621,56 @@
                 probs[m, pair * 2 + half] = soft
                 halves.append(dot(soft.astype(BF16), values))
             ctx[m, :, pl.ds(at, 2 * HEAD_DIM)] = jnp.where(low_half, halves[0], halves[1]).astype(BF16)
+        @pl.when(sec == 0)
+        def _():
+            for cols in chunks(width):
+                put_part(0, m, cols, dot(ctx[m], wfull[me, :, cols]))
+            scatter_start(0, m)
+
+        @pl.when(sec == 1)
+        def _():
+            ctx_all[m, me] = ctx[m]
+            share_start(*contexts(m))
+
+    each_batch(attention)
+
+    def first_norm(m):
+        @pl.when(sec == 0)
+        def _():
+            hidden = entry[m] + scatter_wait(0, m) + bout_ref[...]
+            out, normed, inv_std = norm(hidden, gain1_ref[...], shift1_ref[...])
+            y1[m], n1[m], r1[m] = out, normed, inv_std
+            gath[1, m, mine, :] = out.astype(BF16)
+            gather_start(1, m)
+
+    each_batch(first_norm)
+
+    def whole_norm(m):
+        share_wait(*contexts(m))
         for cols in chunks(width):
-            put_part(0, m, cols, dot(ctx[m], wout_ref[:, cols]))
-        scatter_start(0, m)
-
-    each_batch(attention)
-
-    def first_norm(m):
-        hidden = entry[m] + scatter_wait(0, m) + bout_ref[...]
-        out, normed, inv_std = norm(hidden, gain1_ref[...], shift1_ref[...])
+            part = gath[0, m, :, cols].astype(F32) + bout_ref[:, cols]
+            for source in range(tensor_size):
+                part = part + dot(ctx_all[m, source], wfull[source, :, cols])
+            rs_own[m, :, cols] = part
+        for at in range(0, slot, rows):
+            lines_at = pl.ds(at, rows)
+            out, _, _ = norm(rs_own[m, lines_at, :], gain1_ref[...], shift1_ref[...])
+            gath[1, m, lines_at, :] = out.astype(BF16)
+        out, normed, inv_std = norm(rs_own[m, mine, :], gain1_ref[...], shift1_ref[...])
         y1[m], n1[m], r1[m] = out, normed, inv_std
-        gath[1, m, mine, :] = out.astype(BF16)
-        gather_start(1, m)
-
-    each_batch(first_norm)
 
     for load in loads[2:]:
         load.wait()
 
     def feed_forward(m):
-        gather_wait(1, m)
+        @pl.when(sec == 0)
+        def _():
+            gather_wait(1, m)
+
+        @pl.when(sec == 1)
+        def _():
+            whole_norm(m)
+
         for cols in chunks(units):
             pre = dot(gath[1, m], wup_ref[:, cols]) + bup_ref[:, cols]
             cdf = 0.5 * (1.0 + lax.erf(pre * (1.0 / math.sqrt(2.0))))
@@ -581,20 +684,6 @@
 
     each_batch(feed_forward)
 
-    def second_norm(m):
-        hidden = y1[m] + scatter_wait(1, m) + bdown_ref[...]
-        out, normed, inv_std = norm(hidden, gain2_ref[...], shift2_ref[...])
-        n2[m], r2[m] = normed, inv_std
-        rounded = out.astype(BF16)
-        out_ref[m] = rounded
-
-        @pl.when(sec == 0)
-        def _():
-            sent_up[m] = rounded
-            up_copy(m).start()
-
-    each_batch(second_norm)
-
     def back_entry(m):
         @pl.when(sec == 1)
         def _():
@@ -613,7 +702,35 @@
         gath[2, m, mine, :] = grad.astype(BF16)
         gather_start(2, m)
 
-    each_batch(back_entry)
+    def second_norm(m):
+        hidden = y1[m] + scatter_wait(1, m) + bdown_ref[...]
+        out, normed, inv_std = norm(hidden, gain2_ref[...], shift2_ref[...])
+        n2[m], r2[m] = normed, inv_std
+        rounded = out.astype(BF16)
+        out_ref[m] = rounded
+
+        @pl.when(sec == 0)
+        def _():
+            sent_up[m] = rounded
+            up_copy(m).start()
+
+        @pl.when(sec == 1)
+        def _():
+            back_entry(m)
+
+    each_batch(second_norm)
+
+    @pl.when(sec == 0)
+    def _():
+        for k in range(1, tensor_size):
+            target = {"tensor": lax.rem(me + k, tensor_size)}
+            pl.semaphore_signal(calm_sem, inc=1, device_id=target, device_id_type=MESH)
+        pl.semaphore_wait(calm_sem, tensor_size - 1)
+        share_start(*wide)
+
+    @pl.when(sec == 0)
+    def _():
+        each_batch(back_entry)
 
     def feed_back(m):
         gather_wait(2, m)
@@ -635,9 +752,13 @@
             target[pl.ds(base + rows_at.start, rows_at.size), :] = dot_rows(lhs, rhs).astype(BF16)
 
     weight_grad(act, gath.at[2], pdown)
-    advance(0, 1)
+    advance(0, 0, 1)
     weight_grad(gath.at[1], du, pup)
-    advance(2, 3)
+    advance(0, 2, 3)
+
+    @pl.when(sec == 0)
+    def _():
+        share_wait(*wide)
 
     def first_back(m):
         grad_out = dh2[m] + scatter_wait(2, m)
@@ -646,17 +767,23 @@
         small_acc[4:5, :] += column_sum(grad_out * n1[m])
         small_acc[5:6, :] += column_sum(grad_out)
         dh[m] = grad
-        gath[3, m, mine, :] = grad.astype(BF16)
+        rounded = grad.astype(BF16)
+        gath[3, m, mine, :] = rounded
+        for target in range(tensor_size):
+            dctx_sent[m, target] = dot_last(rounded, wfull[target]).astype(BF16)
+        dctx_all[m, mine, :] = dctx_sent[m, me]
+        for k in range(1, tensor_size):
+            dctx_copy(m, k).start()
         gather_start(3, m)
 
-    each_batch(first_back, lambda m: advance(0, 1) if m == 0 else advance(2, 3))
+    each_batch(first_back, lambda m: advance(0, *AFTER_FIRST[m]))
 
     def attention_back(m):
-        gather_wait(3, m)
+        dctx_wait(m)
         low_half = head_mask()
         for pair in range(pairs):
             at = pair * 2 * HEAD_DIM
-            dctx = dot_last(gath[3, m], wout_ref[pl.ds(at, 2 * HEAD_DIM), :]).astype(BF16)
+            dctx = dctx_all[m, :, pl.ds(at, 2 * HEAD_DIM)]
             queries = qkv[m, :, pl.ds(at, 2 * HEAD_DIM)]
             key_heads = qkv[m, :, pl.ds(local + at, 2 * HEAD_DIM)]
             values = qkv[m, :, pl.ds(2 * local + at, 2 * HEAD_DIM)]
@@ -685,12 +812,21 @@
             put_part(3, m, cols, part)
         scatter_start(3, m)
 
-    each_batch(attention_back, lambda m: advance(1) if m == 0 else None)
-
+    each_batch(attention_back, lambda m: advance(0, *AFTER_ATTENTION[m]))
+
+    def joined_grad():
+        for third in range(3):
+            weight_grad(
+                gath.at[0], dqkv.at[:, :, pl.ds(third * local, local)], pqkv, base=third * width
+            )
+
+    pl.when(sec == 0)(joined_grad)
+    advance(0, 5, 6)
     spread_start(0, small_acc[...])
+    for m in range(batches):
+        gather_wait(3, m)
     weight_grad(ctx, gath.at[3], pout)
-    advance(4)
-    advance(0, 1)
+    advance(0, 4, *AFTER_GRADS)
 
     def last_back(m):
         grad = dh[m] + scatter_wait(3, m)
@@ -701,17 +837,17 @@
             sent_back[m] = grad.astype(BF16)
             back_copy(m).start()
 
-    each_batch(last_back, lambda m: advance(2, 3, 4) if m == 0 else None)
-    for third in range(3):
-        weight_grad(
-            gath.at[0], dqkv.at[:, :, pl.ds(third * local, local)], pqkv, base=third * width
-        )
-    advance(5, 6)
+    each_batch(last_back, lambda m: advance(0, *AFTER_LAST[m]))
+
+    pl.when(sec == 1)(joined_grad)
+    advance(1, 0, 1, 2, 3, 4, 5, 6)
     small_row = lax.broadcasted_iota(jnp.int32, small_acc.shape, 0)
     spread_start(1, jnp.where(small_row < 6, spread_finish(0), small_acc[...]))
     small_step = 1
-    while any(events):
-        advance(0, 1, 2, 3, 4, 5, 6)
+    for part in range(ROUNDS):
+        at = len(TAIL) // ROUNDS
+        advance(0, *TAIL[part * at : (part + 1) * at if part < ROUNDS - 1 else len(TAIL)])
+        advance(1, *TAIL_ONE[part * 14 : part * 14 + 14])
         if small_step < len(SPREAD):
             value = spread_finish(small_step)
             small_step += 1
@@ -719,27 +855,40 @@
                 spread_start(small_step, value)
             else:
                 small_ref[...] = value
-
-    for copy in sends:
-        copy.wait_send()
+    assert not any(events[0]) and not any(events[1])
+
+    for make in sends[0]:
+        make().wait_send()
+    for step in range(len(SPREAD)):
+        index, size = spread_place(step)
+        for k in range(1, size):
+            spread_copy(step, k, index).wait_send()
 
     def drain(m):
         for e in range(4):
             for k in range(1, tensor_size):
-                scatter_copy(e, m, k).wait_send()
                 if e:
+                    scatter_copy(e, m, k).wait_send()
+                if e > 1:
                     gather_copy(e, m, k).wait_send()
+        for k in range(1, tensor_size):
+            dctx_copy(m, k).wait_send()
 
         @pl.when(sec == 0)
         def _():
             up_copy(m).wait_send()
+            for k in range(1, tensor_size):
+                scatter_copy(0, m, k).wait_send()
+                gather_copy(1, m, k).wait_send()
 
         @pl.when(sec == 1)
         def _():
             back_copy(m).wait_send()
+            share_drain(*contexts(m))
 
     for k in range(1, tensor_size):
         gather_copy(0, batches - 1, k).wait_send()
+    share_drain(*wide)
     each_batch(drain)
 
 
@@ -768,7 +917,7 @@
     plan = sum_plan(width, local, units)
     scratch = [
         pltpu.VMEM(wqkv.shape, BF16),
-        pltpu.VMEM(wout.shape, BF16),
+        pltpu.VMEM((tensor_size,) + wout.shape, BF16),
         pltpu.VMEM(wup.shape, BF16),
         pltpu.VMEM(wdown.shape, BF16),
         pltpu.VMEM((4, batches, slot, width), BF16),
@@ -794,6 +943,9 @@
         pltpu.VMEM(shard, BF16),
         pltpu.VMEM(shard, BF16),
         pltpu.VMEM(small_shape, F32),
+        pltpu.VMEM((batches, tensor_size, slot, local), BF16),
+        pltpu.VMEM((batches, tensor_size, rows, local), BF16),
+        pltpu.VMEM((batches, slot, local), BF16),
         pltpu.VMEM((3 * width, local), BF16),
         pltpu.VMEM(wout.shape, BF16),
         pltpu.VMEM(wup.shape, BF16),
@@ -806,11 +958,18 @@
         dma((batches,)),
         dma((batches,)),
         dma((batches,)),
+        dma((others,)),
+        dma((others,)),
+        dma((batches, others)),
+        dma((batches, others)),
+        dma((batches, others)),
+        dma((batches, others)),
         dma((len(plan), 14)),
         dma((len(plan), 14)),
         dma((len(SPREAD), 3)),
         dma((len(SPREAD), 3)),
         dma((4,)),
+        pltpu.SemaphoreType.REGULAR,
     ]
     for axis in SPREAD:
         size = tensor_size if axis == "tensor" else AXES[axis][1]

time: 177 us -> 160 us (0.904)
  Pallas kernels: 176 us -> 159 us
    pallas_call x1, Pallas kernels: 171 us -> 153 us  [run_layer(): pl.pallas_call(functools.partial(layer_kernel, tensor_size, plan), out_sh...]
where the time goes in v4:
time: 160 us; the launch traced here: 159 us
  Pallas kernels  159 us (99%)
    pallas_call x1, Pallas kernels, run_layer(): pl.pallas_call(functools.partial(layer_kernel, tensor_size, plan), out_sh...  153 us
    pallas_call x1, Pallas kernels, unpack(): pl.pallas_call(functools.partial(unpack_kernel, count), out_shape=shapes,...  5.5 us

profile of v4, /device:TPU:1, one launch (start us, length us, event | category | flops | bytes accessed | tf_op | source)
XLA Modules:
  0.0 159.4 jit_solution(4194546263575650996)
XLA Ops:
  0.7 153.1 %layer.1 = (bf16[2,32,1024]{2,1,0:T(8,128)(2,1)S(1)}, f32[2,32,1024]{2,1,0:T(8,128)S(1)}, bf16[3072,256]{1,0:T(8,128)(2,1)S(1)}, bf16[256,1024]{1,0:T(8,128)(2,1...) custom-call(bf16[2,32,1024]{2,1,0:T(8,128)(2,1)} %refs_0_.1, ...), custom_call_target="tpu_custom_call" | custom-call | tf_op jit(solution)/shard_map/layer/pallas_call | solution.py:982
  153.8 5.5 %unpack.1 = (f32[3072,256]{1,0:T(8,128)}, f32[256,1024]{1,0:T(8,128)}, f32[1024,1024]{1,0:T(8,128)}, f32[1024,1024]{1,0:T(8,128)}, bf16[2,32,1024]{2,1,0:T(8,128...) custom-call(bf16[3072,256]{1,0:T(8,128)(2,1)S(1)} %get-tuple-element, ...), custom_call_target="tpu_custom_call" | custom-call | tf_op jit(solution)/shard_map/unpack/pallas_call | solution.py:1032

commit v5 on v4

--- a/solution.py
+++ b/solution.py
@@ -16,11 +16,12 @@
 SPREAD = ("tensor", "core", "y", "x")
 VMEM_BYTES = 52 * 1024 * 1024
 UNPACK_BYTES = 40 * 1024 * 1024
-AFTER_FIRST = ((0,), (1, 2))
+PIECE = 256
+AFTER_FIRST = ((0, 1, 2), ())
 AFTER_ATTENTION = ((3,), ())
-AFTER_GRADS = (0, 1, 2)
-AFTER_LAST = ((3, 5, 6), ())
-TAIL = (4, 0, 1, 2, 3, 5, 6, 0, 4, 5, 1, 6, 2, 0, 4, 3, 5, 1, 0, 6, 4, 5, 2, 3, 1, 4, 5, 2, 0, 6, 3, 0, 1, 4, 2, 5, 1, 6, 2, 3, 5, 4, 6, 3, 4, 6)
+AFTER_GRADS = (0, 1)
+AFTER_LAST = ((5, 2, 3, 6, 4), ())
+TAIL = (0, 1, 2, 3, 5, 6, 2, 4, 5, 0, 6, 1, 2, 3, 4, 5, 0, 6, 2, 1, 4, 5, 3, 6, 0, 1, 5, 2, 3, 2, 6, 4, 0, 4, 1, 0, 3, 1, 6, 5, 3, 6, 5)
 TAIL_ONE = (0, 1, 2, 3, 4, 5, 6) * 8
 ROUNDS = 4
 AXES = {"core": (1, 2), "x": (2, 2), "y": (4, 4)}
@@ -36,11 +37,11 @@
 def sum_plan(width, local, units):
     joined = 3 * width
     return (
-        ("down", 0, units // 2, width, X_FIRST),
+        ("down", 0, units // 2, width, Y_FIRST),
         ("down", units // 2, units // 2, width, Y_FIRST),
-        ("up", 0, width // 2, units, Y_FIRST),
+        ("up", 0, width // 2, units, X_FIRST),
         ("up", width // 2, width // 2, units, Y_FIRST),
-        ("out", 0, local, width, X_FIRST),
+        ("out", 0, local, width, X_FIRST_DIRECT),
         ("qkv", 0, joined // 2, local, X_FIRST),
         ("qkv", joined // 2, joined // 2, local, Y_FIRST),
     )
@@ -165,7 +166,7 @@
         )
 
     def gather_start(e, m):
-        for k in range(1, tensor_size):
+        for k in (2, 1, 3):
             gather_copy(e, m, k).start()
 
     def gather_wait(e, m):
@@ -192,7 +193,7 @@
         )
 
     def scatter_start(e, m):
-        for k in range(1, tensor_size):
+        for k in (2, 1, 3):
             scatter_copy(e, m, k).start()
 
     def scatter_wait(e, m):
@@ -215,7 +216,7 @@
         )
 
     def share_start(whole, ssem, rsem):
-        for k in range(1, tensor_size):
+        for k in (2, 1, 3):
             share_copy(whole, ssem, rsem, k, me).start()
 
     def share_wait(whole, ssem, rsem):
@@ -606,21 +607,26 @@
         col_id = lax.broadcasted_iota(jnp.int32, (slot, slot), 1)
         allowed = ((across == down) & (across >= 0)) | (row_id == col_id)
         low_half = head_mask()
+        def third_of(third, pair):
+            return qkv[m, :, pl.ds(third * local + pair * 2 * HEAD_DIM, 2 * HEAD_DIM)]
+
+        heads = range(2 * pairs)
+        raws = [
+            dot_last(pick(head % 2 == 0, third_of(0, head // 2)), third_of(1, head // 2))
+            for head in heads
+        ]
+        scores = [jnp.where(allowed, raw * scale, -1e30) for raw in raws]
+        peaks = [jnp.max(score, axis=-1, keepdims=True) for score in scores]
+        exps = [jnp.exp(score - peak) for score, peak in zip(scores, peaks)]
+        sums = [jnp.sum(exp, axis=-1, keepdims=True) for exp in exps]
+        softs = [exp / row_sum for exp, row_sum in zip(exps, sums)]
+        halves = [dot(softs[head].astype(BF16), third_of(2, head // 2)) for head in heads]
+        for head in heads:
+            probs[m, head] = softs[head]
         for pair in range(pairs):
-            at = pair * 2 * HEAD_DIM
-            queries = qkv[m, :, pl.ds(at, 2 * HEAD_DIM)]
-            key_heads = qkv[m, :, pl.ds(local + at, 2 * HEAD_DIM)]
-            values = qkv[m, :, pl.ds(2 * local + at, 2 * HEAD_DIM)]
-            halves = []
-            for half in range(2):
-                raw = dot_last(pick(half == 0, queries), key_heads) * scale
-                scores = jnp.where(allowed, raw, -1e30)
-                peak = jnp.max(scores, axis=-1, keepdims=True)
-                exps = jnp.exp(scores - peak)
-                soft = exps / jnp.sum(exps, axis=-1, keepdims=True)
-                probs[m, pair * 2 + half] = soft
-                halves.append(dot(soft.astype(BF16), values))
-            ctx[m, :, pl.ds(at, 2 * HEAD_DIM)] = jnp.where(low_half, halves[0], halves[1]).astype(BF16)
+            both = jnp.where(low_half, halves[2 * pair], halves[2 * pair + 1])
+            ctx[m, :, pl.ds(pair * 2 * HEAD_DIM, 2 * HEAD_DIM)] = both.astype(BF16)
+
         @pl.when(sec == 0)
         def _():
             for cols in chunks(width):
@@ -732,8 +738,24 @@
     def _():
         each_batch(back_entry)
 
+    def weight_grad(left, right, target, base=0):
+        total = batches * slot
+        rhs = right[...].reshape(total, right.shape[-1])
+        for rows_at in chunks(left.shape[-1]):
+            lhs = left[:, :, rows_at].reshape(total, rows_at.size)
+            target[pl.ds(base + rows_at.start, rows_at.size), :] = dot_rows(lhs, rhs).astype(BF16)
+
+    def down_grad():
+        weight_grad(act, gath.at[2], pdown)
+
+    def up_grad():
+        weight_grad(gath.at[1], du, pup)
+
     def feed_back(m):
-        gather_wait(2, m)
+        @pl.when(sec == 1)
+        def _():
+            gather_wait(2, m)
+
         for cols in chunks(units):
             grad = (dot_last(gath[2, m], wdown_ref[cols, :]) * slope[m, :, cols]).astype(BF16)
             du[m, :, cols] = grad
@@ -742,18 +764,22 @@
             put_part(2, m, cols, dot_last(du[m], wup_ref[cols, :]))
         scatter_start(2, m)
 
-    each_batch(feed_back)
-
-    def weight_grad(left, right, target, base=0):
-        total = batches * slot
-        rhs = right[...].reshape(total, right.shape[-1])
-        for rows_at in chunks(left.shape[-1]):
-            lhs = left[:, :, rows_at].reshape(total, rows_at.size)
-            target[pl.ds(base + rows_at.start, rows_at.size), :] = dot_rows(lhs, rhs).astype(BF16)
-
-    weight_grad(act, gath.at[2], pdown)
+    @pl.when(sec == 0)
+    def _():
+        gather_wait(2, 0)
+
+    feed_back(0)
+
+    @pl.when(sec == 0)
+    def _():
+        for m in range(1, batches):
+            gather_wait(2, m)
+        down_grad()
+
     advance(0, 0, 1)
-    weight_grad(gath.at[1], du, pup)
+    for m in range(1, batches):
+        feed_back(m)
+    pl.when(sec == 0)(up_grad)
     advance(0, 2, 3)
 
     @pl.when(sec == 0)
@@ -772,7 +798,7 @@
         for target in range(tensor_size):
             dctx_sent[m, target] = dot_last(rounded, wfull[target]).astype(BF16)
         dctx_all[m, mine, :] = dctx_sent[m, me]
-        for k in range(1, tensor_size):
+        for k in (2, 1, 3):
             dctx_copy(m, k).start()
         gather_start(3, m)
 
@@ -781,27 +807,33 @@
     def attention_back(m):
         dctx_wait(m)
         low_half = head_mask()
-        for pair in range(pairs):
-            at = pair * 2 * HEAD_DIM
-            dctx = dctx_all[m, :, pl.ds(at, 2 * HEAD_DIM)]
-            queries = qkv[m, :, pl.ds(at, 2 * HEAD_DIM)]
-            key_heads = qkv[m, :, pl.ds(local + at, 2 * HEAD_DIM)]
-            values = qkv[m, :, pl.ds(2 * local + at, 2 * HEAD_DIM)]
-            dq, dk, dv = [], [], []
-            for half in range(2):
-                soft = probs[m, pair * 2 + half]
-                dv.append(dot_rows(soft.astype(BF16), dctx))
-                dprob = dot_last(pick(half == 0, dctx), values)
-                dscore = soft * (dprob - jnp.sum(soft * dprob, axis=-1, keepdims=True))
-                dscore = dscore.astype(BF16)
-                dq.append(dot(dscore, key_heads) * scale)
-                dk.append(dot_rows(dscore, queries) * scale)
-            for place, (first, second) in enumerate((dq, dk, dv)):
-                cols = pl.ds(place * local + at, 2 * HEAD_DIM)
-                grad = jnp.where(low_half, first, second).astype(BF16)
-                dqkv[m, :, cols] = grad
-                if place != 1:
-                    to = at if place == 0 else local + at
+        heads = range(2 * pairs)
+
+        def third_of(third, pair):
+            return qkv[m, :, pl.ds(third * local + pair * 2 * HEAD_DIM, 2 * HEAD_DIM)]
+
+        dctx = [dctx_all[m, :, pl.ds(pair * 2 * HEAD_DIM, 2 * HEAD_DIM)] for pair in range(pairs)]
+        dprobs = [
+            dot_last(pick(head % 2 == 0, dctx[head // 2]), third_of(2, head // 2)) for head in heads
+        ]
+        softs = [probs[m, head] for head in heads]
+        means = [
+            jnp.sum(soft * dprob, axis=-1, keepdims=True) for soft, dprob in zip(softs, dprobs)
+        ]
+        dscores = [
+            (soft * (dprob - mean)).astype(BF16)
+            for soft, dprob, mean in zip(softs, dprobs, means)
+        ]
+        dq = [dot(dscores[head], third_of(1, head // 2)) * scale for head in heads]
+        dk = [dot_rows(dscores[head], third_of(0, head // 2)) * scale for head in heads]
+        dv = [dot_rows(softs[head].astype(BF16), dctx[head // 2]) for head in heads]
+        for place_of, parts in enumerate((dq, dk, dv)):
+            for pair in range(pairs):
+                at = pair * 2 * HEAD_DIM
+                grad = jnp.where(low_half, parts[2 * pair], parts[2 * pair + 1]).astype(BF16)
+                dqkv[m, :, pl.ds(place_of * local + at, 2 * HEAD_DIM)] = grad
+                if place_of != 1:
+                    to = at if place_of == 0 else local + at
                     small_acc[7:8, pl.ds(to, 2 * HEAD_DIM)] += column_sum(grad.astype(F32))
         for cols in chunks(width):
             part = dot_last(dqkv[m, :, pl.ds(0, local)], wqkv_ref[0, cols, :])
@@ -825,7 +857,11 @@
     spread_start(0, small_acc[...])
     for m in range(batches):
         gather_wait(3, m)
-    weight_grad(ctx, gath.at[3], pout)
+
+    def out_grad():
+        weight_grad(ctx, gath.at[3], pout)
+
+    pl.when(sec == 0)(out_grad)
     advance(0, 4, *AFTER_GRADS)
 
     def last_back(m):
@@ -839,7 +875,13 @@
 
     each_batch(last_back, lambda m: advance(0, *AFTER_LAST[m]))
 
-    pl.when(sec == 1)(joined_grad)
+    @pl.when(sec == 1)
+    def _():
+        down_grad()
+        up_grad()
+        out_grad()
+        joined_grad()
+
     advance(1, 0, 1, 2, 3, 4, 5, 6)
     small_row = lax.broadcasted_iota(jnp.int32, small_acc.shape, 0)
     spread_start(1, jnp.where(small_row < 6, spread_finish(0), small_acc[...]))
@@ -998,22 +1040,28 @@
     targets, rows_out, grad_out, bqv_out, vectors = (
         refs[:count], refs[count], refs[count + 1], refs[count + 2], refs[count + 3 : count + 10]
     )
-    wides, sem = refs[count + 10 : count + 10 + count], refs[-1]
+    wides, lone, biases, sem = refs[count + 10 : 2 * count + 10], *refs[2 * count + 10 :]
     copies = []
+
+    def write(source, target):
+        copy = pltpu.make_async_copy(source, target, sem.at[len(copies)])
+        copy.start()
+        copies.append(copy)
+
     for source, target, wide in zip(sums, targets, wides):
-        for at in range(0, source.shape[0], 2 * STEP):
-            rows_at = pl.ds(at, min(2 * STEP, source.shape[0] - at))
+        for at in range(0, source.shape[0], PIECE):
+            rows_at = pl.ds(at, PIECE)
             wide[rows_at, :] = source[rows_at, :].astype(F32)
-            copy = pltpu.make_async_copy(wide.at[rows_at], target.at[rows_at], sem.at[len(copies)])
-            copy.start()
-            copies.append(copy)
-    rows_out[...] = rows_ref[...]
-    grad_out[...] = grad_ref[...]
-    for index, vector in enumerate(vectors):
-        vector[...] = small_ref[index : index + 1, :]
+            write(wide.at[rows_at], target.at[rows_at])
+    write(rows_ref, rows_out)
+    write(grad_ref, grad_out)
     half = bqv_out.shape[-1]
     for index in range(2):
-        bqv_out[0, index : index + 1, :] = small_ref[7:8, pl.ds(index * half, half)]
+        biases[0, index : index + 1, :] = small_ref[7:8, pl.ds(index * half, half)]
+    write(biases, bqv_out)
+    for index, vector in enumerate(vectors):
+        lone[index] = small_ref[index : index + 1, :]
+        write(lone.at[index], vector)
     for copy in copies:
         copy.wait()
 
@@ -1022,20 +1070,23 @@
     vmem = pl.BlockSpec(memory_space=pltpu.VMEM)
     count = len(sums)
     vector = jax.ShapeDtypeStruct((1, small.shape[1]), F32)
-    wide = [jax.ShapeDtypeStruct(part.shape, F32) for part in sums]
-    shapes = wide + [
+    shapes = [jax.ShapeDtypeStruct(part.shape, F32) for part in sums] + [
         jax.ShapeDtypeStruct(rows.shape, rows.dtype),
         jax.ShapeDtypeStruct(grad.shape, grad.dtype),
         jax.ShapeDtypeStruct((1, 2, local), F32),
     ] + [vector] * 7
-    pieces = sum(-(-part.shape[0] // (2 * STEP)) for part in sums)
+    pieces = sum(part.shape[0] // PIECE for part in sums) + 10
     return pl.pallas_call(
         functools.partial(unpack_kernel, count),
         out_shape=shapes,
         in_specs=[vmem] * (count + 3),
-        out_specs=[pl.BlockSpec(memory_space=pl.ANY)] * count + [vmem] * 10,
+        out_specs=[pl.BlockSpec(memory_space=pl.ANY)] * (count + 10),
         scratch_shapes=[pltpu.VMEM(part.shape, F32) for part in sums]
-        + [pltpu.SemaphoreType.DMA((pieces,))],
+        + [
+            pltpu.VMEM((7, 1, small.shape[1]), F32),
+            pltpu.VMEM((1, 2, local), F32),
+            pltpu.SemaphoreType.DMA((pieces,)),
+        ],
         compiler_params=pltpu.CompilerParams(vmem_limit_bytes=UNPACK_BYTES),
         name="unpack",
     )(*sums, rows, grad, small)

time: 160 us -> 155 us (0.969)
  Pallas kernels: 159 us -> 154 us
    pallas_call x1, Pallas kernels: 153 us -> 149 us  [run_layer(): pl.pallas_call(functools.partial(layer_kernel, tensor_size, plan), out_sh...]
where the time goes in v5:
time: 155 us; the launch traced here: 154 us
  Pallas kernels  154 us (99%)
    pallas_call x1, Pallas kernels, run_layer(): pl.pallas_call(functools.partial(layer_kernel, tensor_size, plan), out_sh...  149 us
    pallas_call x1, Pallas kernels, unpack(): pl.pallas_call(functools.partial(unpack_kernel, count), out_shape=shapes,...  4.96 us

profile of v5, /device:TPU:1, one launch (start us, length us, event | category | flops | bytes accessed | tf_op | source)
XLA Modules:
  0.0 154.4 jit_solution(2674588011669228369)
XLA Ops:
  0.7 148.7 %layer.1 = (bf16[2,32,1024]{2,1,0:T(8,128)(2,1)S(1)}, f32[2,32,1024]{2,1,0:T(8,128)S(1)}, bf16[3072,256]{1,0:T(8,128)(2,1)S(1)}, bf16[256,1024]{1,0:T(8,128)(2,1...) custom-call(bf16[2,32,1024]{2,1,0:T(8,128)(2,1)} %refs_0_.1, ...), custom_call_target="tpu_custom_call" | custom-call | tf_op jit(solution)/shard_map/layer/pallas_call | solution.py:1024
  149.3 5.0 %unpack.1 = (f32[3072,256]{1,0:T(8,128)}, f32[256,1024]{1,0:T(8,128)}, f32[1024,1024]{1,0:T(8,128)}, f32[1024,1024]{1,0:T(8,128)}, bf16[2,32,1024]{2,1,0:T(8,128...) custom-call(bf16[3072,256]{1,0:T(8,128)(2,1)S(1)} %get-tuple-element, ...), custom_call_target="tpu_custom_call" | custom-call | tf_op jit(solution)/shard_map/unpack/pallas_call | solution.py:1079

commit v6 on v5

--- a/solution.py
+++ b/solution.py
@@ -330,7 +330,7 @@
             return pltpu.make_async_remote_copy(
                 src_ref=source,
                 dst_ref=target,
-                send_sem=sum_ssem.at[c, sem],
+                send_sem=sum_ssem.at[c, sem % 8],
                 recv_sem=sum_rsem.at[c, sem],
                 device_id=dp_peer(axis, k),
                 device_id_type=MESH,
@@ -366,7 +366,7 @@
                 return remote(ref.at[at], landing, RS_SEM[axis], axis, 1)
 
             def begin():
-                send(copy)
+                send((c, RS_SEM[axis]), copy)
 
             def end():
                 copy().wait_recv()
@@ -385,8 +385,8 @@
                 return remote(ref.at[at], landing.at[k - 1], RS_SEM["y"] + k - 1, "y", k)
 
             def begin():
-                for k in range(1, 4):
-                    send(functools.partial(copy, k))
+                for k in (2, 1, 3):
+                    send((c, RS_SEM["y"] + k - 1), functools.partial(copy, k))
 
             def end():
                 for k in range(1, 4):
@@ -420,14 +420,14 @@
 
             def begin():
                 for number in range(4):
-                    send(functools.partial(copy, number))
+                    send((c, RS_SEM["y"] + number), functools.partial(copy, number))
 
             def relay():
                 for number, k, columns_at, out in ((0, 1, high, 4), (2, 3, low, 5)):
                     copy(number).wait_recv()
                     value = at(k, columns_at)[...].astype(F32) + landing[number].astype(F32)
                     landing[out + 2] = value.astype(BF16)
-                    send(functools.partial(copy, out))
+                    send((c, RS_SEM["y"] + out), functools.partial(copy, out))
 
             def end():
                 for number in (1, 3, 4, 5):
@@ -453,7 +453,7 @@
                 return remote(region(step, index), region(step, index), AG_SEM[axis], axis, 1)
 
             return [
-                lambda: send(lambda: copy(place[axis])),
+                lambda: send((c, AG_SEM[axis] % 8), lambda: copy(place[axis])),
                 lambda: copy(1 - place[axis]).wait_recv(),
             ]
 
@@ -463,8 +463,8 @@
                 return remote(part, part, AG_SEM["y"] + k - 1, "y", k)
 
             def begin():
-                for k in range(1, 4):
-                    send(functools.partial(copy, k, 0))
+                for k in (2, 1, 3):
+                    send((c, (AG_SEM["y"] + k - 1) % 8), functools.partial(copy, k, 0))
 
             def end():
                 for k in range(1, 4):
@@ -480,14 +480,14 @@
                 return remote(part, part, AG_SEM["y"] + number, "y", (1, 3, 1, 3)[number])
 
             def begin():
-                send(functools.partial(copy, 0, 0))
-                send(functools.partial(copy, 1, 0))
+                send((c, (AG_SEM["y"] + 0) % 8), functools.partial(copy, 0, 0))
+                send((c, (AG_SEM["y"] + 1) % 8), functools.partial(copy, 1, 0))
 
             def relay():
                 copy(0, 1).wait_recv()
-                send(functools.partial(copy, 2, 1))
+                send((c, (AG_SEM["y"] + 2) % 8), functools.partial(copy, 2, 1))
                 copy(1, 3).wait_recv()
-                send(functools.partial(copy, 3, 3))
+                send((c, (AG_SEM["y"] + 3) % 8), functools.partial(copy, 3, 3))
 
             def end():
                 copy(2, 2).wait_recv()
@@ -515,12 +515,15 @@
         gathers = [forms[axis][1](step) for step, axis in enumerate(order)]
         return join(scatters + gathers[::-1])
 
-    sends, events = ([], []), ([], [])
+    sends, events = ({}, {}), ([], [])
     for section in range(2):
 
-        def send(make, section=section):
+        def send(slot_of, make, section=section):
+            earlier = sends[section].pop(slot_of, None)
+            if earlier is not None:
+                earlier().wait_send()
             make().start()
-            sends[section].append(make)
+            sends[section][slot_of] = make
 
         events[section].extend(sum_events(c, send) for c in range(len(plan)))
 
@@ -774,11 +777,11 @@
     def _():
         for m in range(1, batches):
             gather_wait(2, m)
-        down_grad()
-
-    advance(0, 0, 1)
+
     for m in range(1, batches):
         feed_back(m)
+    pl.when(sec == 0)(down_grad)
+    advance(0, 0, 1)
     pl.when(sec == 0)(up_grad)
     advance(0, 2, 3)
 
@@ -899,7 +902,7 @@
                 small_ref[...] = value
     assert not any(events[0]) and not any(events[1])
 
-    for make in sends[0]:
+    for make in sends[0].values():
         make().wait_send()
     for step in range(len(SPREAD)):
         index, size = spread_place(step)
@@ -1006,7 +1009,7 @@
         dma((batches, others)),
         dma((batches, others)),
         dma((batches, others)),
-        dma((len(plan), 14)),
+        dma((len(plan), 8)),
         dma((len(plan), 14)),
         dma((len(SPREAD), 3)),
         dma((len(SPREAD), 3)),

time: 155 us -> 153 us (0.987)
  Pallas kernels: 154 us -> 152 us
where the time goes in v6:
time: 153 us
  Pallas kernels  152 us (99%)
    pallas_call x1, Pallas kernels, run_layer(): pl.pallas_call(functools.partial(layer_kernel, tensor_size, plan), out_sh...  147 us
    pallas_call x1, Pallas kernels, unpack(): pl.pallas_call(functools.partial(unpack_kernel, count), out_shape=shapes,...  4.96 us

profile of v6, /device:TPU:1, one launch (start us, length us, event | category | flops | bytes accessed | tf_op | source)
XLA Modules:
  0.0 153.2 jit_solution(13807150880666377168)
XLA Ops:
  0.7 147.4 %layer.1 = (bf16[2,32,1024]{2,1,0:T(8,128)(2,1)S(1)}, f32[2,32,1024]{2,1,0:T(8,128)S(1)}, bf16[3072,256]{1,0:T(8,128)(2,1)S(1)}, bf16[256,1024]{1,0:T(8,128)(2,1...) custom-call(bf16[2,32,1024]{2,1,0:T(8,128)(2,1)} %refs_0_.1, ...), custom_call_target="tpu_custom_call" | custom-call | tf_op jit(solution)/shard_map/layer/pallas_call | solution.py:1027
  148.1 5.0 %unpack.1 = (f32[3072,256]{1,0:T(8,128)}, f32[256,1024]{1,0:T(8,128)}, f32[1024,1024]{1,0:T(8,128)}, f32[1024,1024]{1,0:T(8,128)}, bf16[2,32,1024]{2,1,0:T(8,128...) custom-call(bf16[3072,256]{1,0:T(8,128)(2,1)S(1)} %get-tuple-element, ...), custom_call_target="tpu_custom_call" | custom-call | tf_op jit(solution)/shard_map/unpack/pallas_call | solution.py:1082
